TPU v7x, 1024 devices: a whole 4x4x32 slice. The times are simulated.
1024 devices in a mesh: dp: 64 (over z, y_lo), mp: 4 (over x), blk: 4 (over y_hi, core).
Axes of the slice: x: 4, y: 4 (y_hi: 2, y_lo: 2; y = y_hi * 2 + y_lo), z: 32, core: 2. Of those that a mesh axis runs over, the one named last changes fastest.
Arguments:
- activations: bfloat16 [98304, 2560], P('dp', 'blk'), may hold values from -13 to 13
- cotangent: bfloat16 [98304, 2560], P('dp', 'mp'), may hold values from -13 to 13
Outputs:
- update: float32 [4, 640, 2560], P('blk', 'dp', 'mp')
All inputs are finite; a program needn't handle non-finite values.
Results may differ from a plain program's by a relative error of at most 0.007.
Values may be sent and summed in bfloat16 or wider, within the bound.
No kernel may reach another device: no remote copies, remote signals or barrier semaphores. Data moves between devices by JAX's collectives and lax.ppermute only.
A program may use at most 32 MiB of HBM per device.

v0:
```python
import math

import jax
import jax.numpy as jnp
from jax import lax
from jax.sharding import PartitionSpec as P

ridge_shift = 0.05
tiny_shift = 1e-12


def shortened(array):
    return jax.tree.map(lambda a: a.astype(jnp.bfloat16) if a.dtype == jnp.float32 else a, array)


def broadcast(block, axis, source):
    block = jnp.where(lax.axis_index(axis) == source, block, jnp.zeros_like(block))
    return lax.psum(block, axis)


def inverse_root(statistic):
    highest = lax.Precision.HIGHEST
    extent = statistic.shape[0]
    identity = jnp.eye(extent, dtype=jnp.float32)
    frobenius = jnp.sqrt(jnp.sum(statistic * statistic) + tiny_shift)
    shifted = statistic / frobenius + ridge_shift * identity
    squared = jnp.dot(shifted, shifted, precision=highest, preferred_element_type=jnp.float32)
    factor = (5.0 * identity - shifted) / 4.0
    factor_two = (25.0 * identity - 10.0 * shifted + squared) / 16.0
    factor_four = jnp.dot(
        factor_two, factor_two, precision=highest, preferred_element_type=jnp.float32
    )
    factor_shifted = (5.0 * shifted - squared) / 4.0
    product = jnp.dot(
        factor_four, factor_shifted, precision=highest, preferred_element_type=jnp.float32
    )
    return ((5.0 * factor - product) / 4.0).astype(jnp.bfloat16)


def per_device(activations, cotangent):
    dp_count = lax.axis_size("dp")
    dp_index = lax.axis_index("dp")
    extent = cotangent.shape[1]
    slab_rows = extent // dp_count
    scaling = 1.0 / math.sqrt(activations.shape[0] * dp_count)
    product = lax.dot_general(
        activations, cotangent, (((0,), (0,)), ((), ())), preferred_element_type=jnp.float32
    )
    gradient = lax.psum(product * scaling, "dp").astype(jnp.bfloat16)

    def skipped():
        return jnp.zeros((extent, extent), jnp.bfloat16)

    def left_side():
        statistic = lax.dot_general(
            gradient, gradient, (((1,), (1,)), ((), ())), preferred_element_type=jnp.float32
        )
        return inverse_root(statistic)

    def right_side():
        statistic = lax.dot_general(
            gradient, gradient, (((0,), (0,)), ((), ())), preferred_element_type=jnp.float32
        )
        return inverse_root(statistic)

    left_owner = 0
    right_owner = 1
    duty = jnp.where(dp_index == left_owner, 1, jnp.where(dp_index == right_owner, 2, 0))
    local_root = lax.switch(duty, [skipped, left_side, right_side])
    left_root, right_root = [
        jax.tree.map(
            lambda part, own: part.astype(own.dtype),
            jax.tree.map(lambda part: broadcast(part, "dp", owner), shortened(local_root)),
            local_root,
        )
        for owner in (left_owner, right_owner)
    ]
    left_rows = lax.dynamic_slice_in_dim(left_root, dp_index * slab_rows, slab_rows, 0)
    left_part = jnp.dot(left_rows, gradient, preferred_element_type=jnp.float32).astype(
        jnp.bfloat16
    )
    direction = jnp.dot(left_part, right_root, preferred_element_type=jnp.float32)
    widened = gradient.astype(jnp.float32)
    gradient_norm = jnp.sum(widened * widened)
    direction_norm = lax.psum(jnp.sum(direction * direction), "dp")
    grafted = direction * jnp.sqrt(gradient_norm / (direction_norm + tiny_shift))
    return grafted[None]


def solution(mesh):
    placed = (P("dp", "blk"), P("dp", "mp"))
    return jax.shard_map(
        per_device, mesh=mesh, in_specs=placed, out_specs=P("blk", "dp", "mp"), check_vma=False
    )
```

profile of v0, /device:TPU:4, one launch (start us, length us, event | category | flops | bytes accessed | tf_op | source)
XLA Modules:
  0.0 942.5 jit_solution(7614318485486380228)
XLA Ops:
  6.5 0.0 copy-start
  6.5 0.0 all-reduce.4.cloned.1.call-start
  6.5 1.5 copy-done
  8.1 4.5 convolution_multiply_fusion
  12.6 275.0 %all-reduce.5 = bf16[640,640]{1,0:T(8,128)(2,1)S(1)} all-reduce(f32[640,640]{1,0:T(8,128)} %convolution_multiply_fusion), channel_id=1, replica_groups=mesh['dp'=64,'mp'=4,'blk'=4] {'dp'}, use_global_device_ids=true, to_apply=%region_0.0 | all-reduce | flops 409600 | bytes 2457600 | tf_op jit(solution)/shard_map/psum | solution.py:49
  287.6 21.0 %conditional.1 = (bf16[640,640]{1,0:T(8,128)(2,1)}) conditional(s32[]{:T(128)} %clamp.3, () %tuple.14, bf16[640,640]{1,0:T(8,128)(2,1)S(1)} %all-reduce.5, bf16[640,640]{1,0:T(8,128)(2,1)S(1)} %all-reduce.5), branch_computations={%region_1.2_spmd, %region_2.4_spmd, %region_4.6_spmd} | conditional | flops 9974579200 | bytes 22937672 | solution.py:69
  287.8 2.7 multiply_reduce_fusion
  291.0 0.0 copy-start.1
  291.1 6.8 fusion.24
  297.9 0.0 copy-done.1
  297.9 5.0 fusion.4
  302.9 5.7 multiply_convert_fusion
  308.6 2.5 broadcast_select_fusion.1
  311.1 0.0 all-reduce.4.cloned.1.call-update
  311.1 1.0 multiply_reduce_fusion.2
  312.1 498.1 %all-reduce.4.cloned.1.call-done = (bf16[640,640]{1,0:T(8,128)(2,1)}, bf16[640,640]{1,0:T(8,128)(2,1)}) async-done(((bf16[640,640]{1,0:T(8,128)(2,1)}, bf16[640,640]{1,0:T(8,128)(2,1)}), (bf16[640,640]{1,0:T(8,128)(2,1)}, bf16[640,640]{1,0:T(8,128)(2,1)})) %all-reduce.4.cloned.1.call-update) | async-done | bytes 1638416 | tf_op jit(solution)/shard_map/psum | solution.py:18
  810.2 2.2 multiply_reduce_fusion.3
  812.4 121.4 %psum.31 = f32[]{:T(128)} all-reduce(f32[]{:T(128)} %get-tuple-element.19), channel_id=1, replica_groups=mesh['dp'=64,'mp'=4,'blk'=4] {'dp'}, use_global_device_ids=true, to_apply=%region_10.11 | all-reduce | flops 1 | bytes 8 | tf_op jit(solution)/shard_map/psum | solution.py:85
  935.0 0.6 copy.3
  (1 shorter events, 0.0 us)
Async XLA Ops:
  6.5 1.5 copy-start
  6.5 803.7 %all-reduce.4.cloned.1.call-start = ((), (), s32[]{:S(2)}) async-start(), calls=%async_computation | async-start | bytes 3276800 | tf_op jit(solution)/shard_map/psum | solution.py:18
  291.0 6.8 copy-start.1
Sparse Core Ops, SparseCore 0:
  311.2 498.9 all-reduce.3
where the time goes:
time: 943 us; the launch traced here: 942 us
  waiting for transfers between devices  498 us (53%)
  blocking collectives  396 us (42%)
  matrix products  26.8 us (3%)
  between operations  14.7 us (2%)
    psum x1, waiting for transfers between devices, broadcast(): return lax.psum(block, axis)  498 us
    psum x1, blocking collectives, per_device(): gradient = lax.psum(product * scaling, 'dp').astype(jnp.bfloat16)  275 us
    psum x1, blocking collectives, per_device(): direction_norm = lax.psum(jnp.sum(direction * direction), 'dp')  121 us
  transfers between devices with their start and end apart: 1, of which 1 were waited for; matrix products, arithmetic and copies ran while one was open for 0% of the time, Pallas kernels for 0%

commit v1 on v0

v1 whole, which is shorter than its diff:
```python
import math

import jax
import jax.numpy as jnp
import numpy as np
from jax import lax
from jax.experimental import pallas as pl
from jax.experimental.pallas import tpu as pltpu
from jax.sharding import PartitionSpec as P

ridge_shift = 0.05
tiny_shift = 1e-12
chunk = 128


def root_coefficients():
    poly = np.polynomial.Polynomial
    shifted = poly([ridge_shift, 1.0])
    factor = (5.0 - shifted) / 4.0
    return [float(c) for c in ((5.0 * factor - factor**5 * shifted) / 4.0).coef]


def precondition_kernel(
    start_ref, g_ref, out_ref, stat, one, two, two_wide, three, mixed, base, wide, narrow, direction
):
    q = root_coefficients()
    extent = g_ref.shape[0]
    slices = [pl.ds(i * chunk, chunk) for i in range(extent // chunk)]

    def product(left, right):
        return jnp.dot(left, right, preferred_element_type=jnp.float32)

    total = jnp.float32(0.0)
    for rows in slices:
        part = lax.dot_general(
            g_ref[:, rows], g_ref[...], (((0,), (0,)), ((), ())), preferred_element_type=jnp.float32
        )
        stat[rows, :] = part
        total += jnp.sum(part * part)
    inverse = 1.0 / jnp.sqrt(total + tiny_shift)
    for rows in slices:
        part = stat[rows, :] * inverse
        stat[rows, :] = part
        one[rows, :] = part.astype(jnp.bfloat16)
    for rows in slices:
        part = product(one[rows, :], one[...])
        two_wide[rows, :] = part
        two[rows, :] = part.astype(jnp.bfloat16)
    for rows in slices:
        cubed = product(one[rows, :], two[...])
        first, second = stat[rows, :], two_wide[rows, :]
        three[rows, :] = cubed.astype(jnp.bfloat16)
        base[rows, :] = q[1] * first + q[2] * second + q[3] * cubed
        mixed[rows, :] = (q[4] * first + q[5] * second + q[6] * cubed).astype(jnp.bfloat16)
    for rows in slices:
        part = base[rows, :] + product(three[rows, :], mixed[...])
        wide[rows, :] = part
        narrow[rows, :] = part.astype(jnp.bfloat16)
    for rows in slices:
        part = (2.0 * q[0]) * wide[rows, :] + product(narrow[rows, :], narrow[...])
        one[rows, :] = part.astype(jnp.bfloat16)
    gradient_norm, direction_norm = jnp.float32(0.0), jnp.float32(0.0)
    for rows in slices:
        widened = g_ref[rows, :].astype(jnp.float32)
        part = (q[0] * q[0]) * widened + product(g_ref[rows, :], one[...])
        direction[rows, :] = part
        gradient_norm += jnp.sum(widened * widened)
        direction_norm += jnp.sum(part * part)
    scale = jnp.sqrt(gradient_norm / (direction_norm + tiny_shift))
    for i in range(out_ref.shape[0]):
        out_ref[pl.ds(i, 1), :] = direction[pl.ds(start_ref[0] + i, 1), :] * scale


def precondition(gradient, start, slab_rows):
    extent = gradient.shape[0]
    square = (extent, extent)
    f32, bf16 = pltpu.VMEM(square, jnp.float32), pltpu.VMEM(square, jnp.bfloat16)
    return pl.pallas_call(
        precondition_kernel,
        out_shape=jax.ShapeDtypeStruct((slab_rows, extent), jnp.float32),
        in_specs=[
            pl.BlockSpec(memory_space=pltpu.SMEM),
            pl.BlockSpec(memory_space=pltpu.VMEM),
        ],
        out_specs=pl.BlockSpec(memory_space=pltpu.VMEM),
        scratch_shapes=[f32, bf16, bf16, f32, bf16, bf16, f32, f32, bf16, f32],
        compiler_params=pltpu.CompilerParams(vmem_limit_bytes=40 * 1024 * 1024),
        cost_estimate=pl.CostEstimate(
            flops=12 * extent**3, bytes_accessed=2 * extent * extent, transcendentals=2
        ),
    )(start, gradient)


def stage_groups(count):
    near = [[4 * k + r for r in range(4)] for k in range(count // 4)]
    middle = [[16 * b + 4 * j + r for j in range(4)] for b in range(count // 16) for r in range(4)]
    far = [[16 * b + c for b in range(count // 16)] for c in range(16)]
    return near, middle, far


def exchange(parts, groups):
    return lax.all_to_all(parts, "dp", 0, 0, axis_index_groups=groups)


def summed(parts):
    return jnp.sum(parts.astype(jnp.float32), axis=0).astype(jnp.bfloat16)


def spread(part, groups):
    count = len(groups[0])
    return exchange(jnp.broadcast_to(part[None], (count,) + part.shape), groups)


def per_device(activations, cotangent):
    dp_count = lax.axis_size("dp")
    dp_index = lax.axis_index("dp")
    extent = cotangent.shape[1]
    slab_rows = extent // dp_count
    scaling = 1.0 / math.sqrt(activations.shape[0] * dp_count)
    near, middle, far = stage_groups(dp_count)
    with jax.named_scope("product"):
        product = lax.dot_general(
            activations, cotangent, (((0,), (0,)), ((), ())), preferred_element_type=jnp.float32
        )
        part = (product * scaling).astype(jnp.bfloat16)
    with jax.named_scope("near_sum"):
        part = summed(exchange(part.reshape(4, extent // 4, extent), near))
    with jax.named_scope("middle_sum"):
        part = summed(exchange(part.reshape(4, extent // 16, extent), middle))
    with jax.named_scope("far_sum"):
        part = summed(spread(part, far))
    with jax.named_scope("middle_gather"):
        part = spread(part, middle).reshape(extent // 4, extent)
    with jax.named_scope("near_gather"):
        gradient = spread(part, near).reshape(extent, extent)
    with jax.named_scope("precondition"):
        start = jnp.reshape(dp_index * slab_rows, (1,)).astype(jnp.int32)
        return precondition(gradient, start, slab_rows)[None]


def solution(mesh):
    placed = (P("dp", "blk"), P("dp", "mp"))
    return jax.shard_map(
        per_device, mesh=mesh, in_specs=placed, out_specs=P("blk", "dp", "mp"), check_vma=False
    )
```

time: 943 us -> 136 us (0.14)
  the two profiles are of different devices: /device:TPU:4 before, /device:TPU:2 now
where the time goes in v1:
time: 136 us; the launch traced here: 135 us
  blocking collectives  111 us (82%)
  waiting for transfers between devices  8.16 us (6%)
  Pallas kernels  6.13 us (5%)
  starting transfers between devices  3.5 us (3%)
  matrix products  3.28 us (2%)
  local copies, waits for them, and re-layouts  3.17 us (2%)
    all_to_all x4, blocking collectives, exchange(): return lax.all_to_all(parts, 'dp', 0, 0, axis_index_groups=groups)  111 us
    all_to_all x1, waiting for transfers between devices, exchange(): return lax.all_to_all(parts, 'dp', 0, 0, axis_index_groups=groups)  8.16 us
    pallas_call x1, Pallas kernels, precondition(): pl.pallas_call(precondition_kernel, out_shape=jax.ShapeDtypeStruct((slab_...  6.13 us
    all_to_all x1, starting transfers between devices, exchange(): return lax.all_to_all(parts, 'dp', 0, 0, axis_index_groups=groups)  3.5 us
    dot_general x1, matrix products, per_device(): lax.dot_general(activations, cotangent, (((0,), (0,)), ((), ())), preferr...  3.28 us
  transfers between devices with their start and end apart: 1, of which 1 were waited for; matrix products, arithmetic and copies ran while one was open for 0% of the time, Pallas kernels for 0%

profile of v1, /device:TPU:2, one launch (start us, length us, event | category | flops | bytes accessed | tf_op | source)
XLA Modules:
  0.0 135.4 jit_solution(3358522040276752012)
XLA Ops:
  0.0 0.0 copy-start
  0.0 1.5 %copy-done = bf16[1536,640]{1,0:T(8,128)(2,1)S(1)} copy-done((bf16[1536,640]{1,0:T(8,128)(2,1)S(1)}, bf16[1536,640]{1,0:T(8,128)(2,1)}, u32[]{:S(2)}) %copy-start) | copy-done | bytes 1966104
  1.5 3.3 %multiply_convert_fusion = bf16[640,640]{1,0:T(8,128)(2,1)S(1)} fusion(bf16[1536,640]{1,0:T(8,128)(2,1)S(1)} %copy-done, bf16[1536,640]{1,0:T(8,128)(2,1)} %param.3), kind=kOutput, calls=%fused_computation | convolution fusion | flops 1259110400 | bytes 4751360 | tf_op jit(solution)/shard_map/product/dot_general | solution.py:122
  4.8 15.9 %all_to_all.25 = bf16[4,160,640]{2,1,0:T(8,128)(2,1)S(1)} all-to-all(bf16[4,160,640]{2,1,0:T(8,128)(2,1)S(1)} %bitcast.11), channel_id=1, replica_groups={{0,16,32,48},{64,80,96,112},{128,144,160,176},{192,208,224,240},{256,27..., dimensions={0} | all-to-all | bytes 1638400 | tf_op jit(solution)/shard_map/near_sum/all_to_all | solution.py:102
  20.8 0.1 reduce_sum.36
  20.9 24.7 %all_to_all.26 = bf16[4,40,640]{2,1,0:T(8,128)(2,1)S(1)} all-to-all(bf16[4,40,640]{2,1,0:T(8,128)(2,1)S(1)} %bitcast.10), channel_id=1, replica_groups={{0,64,128,192},{16,80,144,208},{32,96,160,224},{48,112,176,240},{256,32..., dimensions={0} | all-to-all | bytes 409600 | tf_op jit(solution)/shard_map/middle_sum/all_to_all | solution.py:102
  45.7 49.8 %all_to_all.27 = bf16[4,40,640]{2,1,0:T(8,128)(2,1)S(1)} all-to-all(bf16[4,40,640]{2,1,0:T(8,128)(2,1)S(1)} %broadcast_in_dim.10), channel_id=1, replica_groups={{0,256,512,768},{16,272,528,784},{32,288,544,800},{48,304,560,816},{64,..., dimensions={0} | all-to-all | bytes 409600 | tf_op jit(solution)/shard_map/far_sum/all_to_all | solution.py:102
  95.6 20.4 %all_to_all.28 = bf16[4,40,640]{2,1,0:T(8,128)(2,1)S(1)} all-to-all(bf16[4,40,640]{2,1,0:T(8,128)(2,1)S(1)} %broadcast_in_dim.11), channel_id=1, replica_groups={{0,64,128,192},{16,80,144,208},{32,96,160,224},{48,112,176,240},{256,32..., dimensions={0} | all-to-all | bytes 409600 | tf_op jit(solution)/shard_map/middle_gather/all_to_all | solution.py:102
  116.0 1.0 broadcast_in_dim.25
  116.9 3.5 %all-to-all-start.4 = ((bf16[4,160,640]{2,1,0:T(8,128)(2,1)}), bf16[4,160,640]{2,1,0:T(8,128)(2,1)S(1)}, u32[]{:S(2)}, u32[]{:S(2)}) async-start(bf16[4,160,640]{2,1,0:T(8,128)(2,1)} %broadcast_in_dim.25), calls=%async_computation.4 | async-start | bytes 1638400 | tf_op jit(solution)/shard_map/near_gather/all_to_all | solution.py:102
  120.4 8.2 %all-to-all-done.4 = bf16[4,160,640]{2,1,0:T(8,128)(2,1)S(1)} async-done(((bf16[4,160,640]{2,1,0:T(8,128)(2,1)}), bf16[4,160,640]{2,1,0:T(8,128)(2,1)S(1)}, u32[]{:S(2)}, u32[]{:S(2)}) %all-to-all-start.4) | async-done | bytes 819232 | tf_op jit(solution)/shard_map/near_gather/all_to_all | solution.py:102
  128.6 6.1 %precondition.1 = f32[10,640]{1,0:T(8,128)S(1)} custom-call(s32[1]{0:T(128)} %bitcast.start_ref, bf16[640,640]{1,0:T(8,128)(2,1)S(1)} %bitcast.8), custom_call_target="tpu_custom_call" | custom-call | flops 3145728000 | bytes 819200 | tf_op jit(solution)/shard_map/precondition/pallas_call | solution.py:78
  134.7 0.6 copy.4
  (4 shorter events, 0.1 us)
Async XLA Ops:
  0.0 1.5 %copy-start = (bf16[1536,640]{1,0:T(8,128)(2,1)S(1)}, bf16[1536,640]{1,0:T(8,128)(2,1)}, u32[]{:S(2)}) copy-start(bf16[1536,640]{1,0:T(8,128)(2,1)} %param.2) | copy-start | bytes 5898244
  116.9 11.7 %all-to-all-start.4 = ((bf16[4,160,640]{2,1,0:T(8,128)(2,1)}), bf16[4,160,640]{2,1,0:T(8,128)(2,1)S(1)}, u32[]{:S(2)}, u32[]{:S(2)}) async-start(bf16[4,160,640]{2,1,0:T(8,128)(2,1)} %broadcast_in_dim.25), calls=%async_computation.4 | async-start | bytes 1638400 | tf_op jit(solution)/shard_map/near_gather/all_to_all | solution.py:102

commit v2 on v1

--- a/solution.py
+++ b/solution.py
@@ -10,7 +10,10 @@
 
 ridge_shift = 0.05
 tiny_shift = 1e-12
-chunk = 128
+chunk = 640
+axes = ("dp", "mp", "blk")
+core_shift = 9
+stage_bits = (((0, 1), (2, 3), (4, 5)), ((0, 1), (2, 3), (4, 5)))
 
 
 def root_coefficients():
@@ -18,6 +21,10 @@
     shifted = poly([ridge_shift, 1.0])
     factor = (5.0 - shifted) / 4.0
     return [float(c) for c in ((5.0 * factor - factor**5 * shifted) / 4.0).coef]
+
+
+def folded(part):
+    return jnp.sum(part.reshape(part.shape[0] // 8, 8, part.shape[1]), axis=0)
 
 
 def precondition_kernel(
@@ -30,25 +37,22 @@
     def product(left, right):
         return jnp.dot(left, right, preferred_element_type=jnp.float32)
 
-    total = jnp.float32(0.0)
+    total = jnp.zeros((8, extent), jnp.float32)
     for rows in slices:
         part = lax.dot_general(
             g_ref[:, rows], g_ref[...], (((0,), (0,)), ((), ())), preferred_element_type=jnp.float32
         )
         stat[rows, :] = part
-        total += jnp.sum(part * part)
-    inverse = 1.0 / jnp.sqrt(total + tiny_shift)
+        one[rows, :] = part.astype(jnp.bfloat16)
+        total += folded(part * part)
+    inverse = 1.0 / jnp.sqrt(jnp.sum(total) + tiny_shift)
     for rows in slices:
-        part = stat[rows, :] * inverse
-        stat[rows, :] = part
-        one[rows, :] = part.astype(jnp.bfloat16)
-    for rows in slices:
-        part = product(one[rows, :], one[...])
+        part = product(one[rows, :], one[...]) * (inverse * inverse)
         two_wide[rows, :] = part
         two[rows, :] = part.astype(jnp.bfloat16)
     for rows in slices:
-        cubed = product(one[rows, :], two[...])
-        first, second = stat[rows, :], two_wide[rows, :]
+        cubed = product(one[rows, :], two[...]) * inverse
+        first, second = stat[rows, :] * inverse, two_wide[rows, :]
         three[rows, :] = cubed.astype(jnp.bfloat16)
         base[rows, :] = q[1] * first + q[2] * second + q[3] * cubed
         mixed[rows, :] = (q[4] * first + q[5] * second + q[6] * cubed).astype(jnp.bfloat16)
@@ -59,16 +63,17 @@
     for rows in slices:
         part = (2.0 * q[0]) * wide[rows, :] + product(narrow[rows, :], narrow[...])
         one[rows, :] = part.astype(jnp.bfloat16)
-    gradient_norm, direction_norm = jnp.float32(0.0), jnp.float32(0.0)
+    gradient_norm = jnp.zeros((8, extent), jnp.float32)
+    direction_norm = jnp.zeros((8, extent), jnp.float32)
     for rows in slices:
         widened = g_ref[rows, :].astype(jnp.float32)
         part = (q[0] * q[0]) * widened + product(g_ref[rows, :], one[...])
         direction[rows, :] = part
-        gradient_norm += jnp.sum(widened * widened)
-        direction_norm += jnp.sum(part * part)
-    scale = jnp.sqrt(gradient_norm / (direction_norm + tiny_shift))
+        gradient_norm += folded(widened * widened)
+        direction_norm += folded(part * part)
+    scale = jnp.sqrt(jnp.sum(gradient_norm) / (jnp.sum(direction_norm) + tiny_shift))
     for i in range(out_ref.shape[0]):
-        out_ref[pl.ds(i, 1), :] = direction[pl.ds(start_ref[0] + i, 1), :] * scale
+        out_ref[i] = direction[pl.ds(start_ref[0] + i, 1), :] * scale
 
 
 def precondition(gradient, start, slab_rows):
@@ -77,7 +82,7 @@
     f32, bf16 = pltpu.VMEM(square, jnp.float32), pltpu.VMEM(square, jnp.bfloat16)
     return pl.pallas_call(
         precondition_kernel,
-        out_shape=jax.ShapeDtypeStruct((slab_rows, extent), jnp.float32),
+        out_shape=jax.ShapeDtypeStruct((slab_rows, 1, extent), jnp.float32),
         in_specs=[
             pl.BlockSpec(memory_space=pltpu.SMEM),
             pl.BlockSpec(memory_space=pltpu.VMEM),
@@ -91,15 +96,31 @@
     )(start, gradient)
 
 
-def stage_groups(count):
-    near = [[4 * k + r for r in range(4)] for k in range(count // 4)]
-    middle = [[16 * b + 4 * j + r for j in range(4)] for b in range(count // 16) for r in range(4)]
-    far = [[16 * b + c for b in range(count // 16)] for c in range(16)]
-    return near, middle, far
+def stage_groups():
+    count, n_mp, n_blk = (lax.axis_size(axis) for axis in axes)
+    rings = count // 2
+
+    def placed(stage):
+        groups = []
+        for mp in range(n_mp):
+            for blk in range(n_blk):
+                core = blk % 2
+                low, high = (1 << bit for bit in stage_bits[core][stage])
+                for base in range(count):
+                    if base & (low | high):
+                        continue
+                    members = [base, base | low, base | high, base | low | high]
+                    groups.append([
+                        (((v // 2 + core_shift * core) % rings * 2 + v % 2) * n_mp + mp) * n_blk + blk
+                        for v in members
+                    ])
+        return groups
+
+    return [placed(stage) for stage in range(3)]
 
 
 def exchange(parts, groups):
-    return lax.all_to_all(parts, "dp", 0, 0, axis_index_groups=groups)
+    return lax.all_to_all(parts, axes, 0, 0, axis_index_groups=groups)
 
 
 def summed(parts):
@@ -117,7 +138,7 @@
     extent = cotangent.shape[1]
     slab_rows = extent // dp_count
     scaling = 1.0 / math.sqrt(activations.shape[0] * dp_count)
-    near, middle, far = stage_groups(dp_count)
+    near, middle, far = stage_groups()
     with jax.named_scope("product"):
         product = lax.dot_general(
             activations, cotangent, (((0,), (0,)), ((), ())), preferred_element_type=jnp.float32
@@ -128,14 +149,14 @@
     with jax.named_scope("middle_sum"):
         part = summed(exchange(part.reshape(4, extent // 16, extent), middle))
     with jax.named_scope("far_sum"):
-        part = summed(spread(part, far))
+        part = summed(lax.all_gather(part, axes, axis_index_groups=far))
     with jax.named_scope("middle_gather"):
         part = spread(part, middle).reshape(extent // 4, extent)
     with jax.named_scope("near_gather"):
         gradient = spread(part, near).reshape(extent, extent)
     with jax.named_scope("precondition"):
         start = jnp.reshape(dp_index * slab_rows, (1,)).astype(jnp.int32)
-        return precondition(gradient, start, slab_rows)[None]
+        return jnp.transpose(precondition(gradient, start, slab_rows), (1, 0, 2))
 
 
 def solution(mesh):

time: 136 us -> 125 us (0.919)
  the two profiles are of different devices: /device:TPU:2 before, /device:TPU:1 now
where the time goes in v2:
time: 125 us
  blocking collectives  98.7 us (79%)
  waiting for transfers between devices  10.5 us (8%)
  Pallas kernels  5.67 us (5%)
  starting transfers between devices  3.94 us (3%)
  matrix products  3.28 us (3%)
  local copies, waits for them, and re-layouts  2.52 us (2%)
    all_to_all x3, blocking collectives, exchange(): return lax.all_to_all(parts, axes, 0, 0, axis_index_groups=groups)  64.7 us
    all_gather x1, blocking collectives, per_device(): part = summed(lax.all_gather(part, axes, axis_index_groups=far))  34 us
    all_to_all x1, waiting for transfers between devices, exchange(): return lax.all_to_all(parts, axes, 0, 0, axis_index_groups=groups)  10.5 us
    pallas_call x1, Pallas kernels, precondition(): pl.pallas_call(precondition_kernel, out_shape=jax.ShapeDtypeStruct((slab_...  5.67 us
    all_to_all x1, starting transfers between devices, exchange(): return lax.all_to_all(parts, axes, 0, 0, axis_index_groups=groups)  3.94 us
    dot_general x1, matrix products, per_device(): lax.dot_general(activations, cotangent, (((0,), (0,)), ((), ())), preferr...  3.28 us
  transfers between devices with their start and end apart: 1, of which 1 were waited for; matrix products, arithmetic and copies ran while one was open for 0% of the time, Pallas kernels for 0%

profile of v2, /device:TPU:1, one launch (start us, length us, event | category | flops | bytes accessed | tf_op | source)
XLA Modules:
  0.0 124.8 jit_solution(17910843368661197247)
XLA Ops:
  0.0 0.0 copy-start
  0.0 1.5 %copy-done = bf16[1536,640]{1,0:T(8,128)(2,1)S(1)} copy-done((bf16[1536,640]{1,0:T(8,128)(2,1)S(1)}, bf16[1536,640]{1,0:T(8,128)(2,1)}, u32[]{:S(2)}) %copy-start) | copy-done | bytes 1966104
  1.5 3.3 %multiply_convert_fusion = bf16[640,640]{1,0:T(8,128)(2,1)S(1)} fusion(bf16[1536,640]{1,0:T(8,128)(2,1)S(1)} %copy-done, bf16[1536,640]{1,0:T(8,128)(2,1)} %param.3), kind=kOutput, calls=%fused_computation | convolution fusion | flops 1259110400 | bytes 4751360 | tf_op jit(solution)/shard_map/product/dot_general | solution.py:143
  4.8 28.4 %all_to_all.20 = bf16[4,160,640]{2,1,0:T(8,128)(2,1)S(1)} all-to-all(bf16[4,160,640]{2,1,0:T(8,128)(2,1)S(1)} %bitcast.11), channel_id=1, replica_groups={{0,16,32,48},{64,80,96,112},{128,144,160,176},{192,208,224,240},{256,27..., dimensions={0} | all-to-all | bytes 1638400 | tf_op jit(solution)/shard_map/near_sum/all_to_all | solution.py:123
  33.2 0.1 reduce_sum.36
  33.4 17.2 %all_to_all.21 = bf16[4,40,640]{2,1,0:T(8,128)(2,1)S(1)} all-to-all(bf16[4,40,640]{2,1,0:T(8,128)(2,1)S(1)} %bitcast.10), channel_id=1, replica_groups={{0,64,128,192},{16,80,144,208},{32,96,160,224},{48,112,176,240},{256,32..., dimensions={0} | all-to-all | bytes 409600 | tf_op jit(solution)/shard_map/middle_sum/all_to_all | solution.py:123
  50.6 34.0 %all-gather = bf16[160,640]{1,0:T(8,128)(2,1)S(1)} all-gather(bf16[40,640]{1,0:T(8,128)(2,1)S(1)} %reduce_sum.37), channel_id=2, replica_groups={{0,256,512,768},{16,272,528,784},{32,288,544,800},{48,304,560,816},{64,..., dimensions={0}, use_global_device_ids=true | all-gather | bytes 256000 | tf_op jit(solution)/shard_map/far_sum/all_gather | solution.py:152
  84.6 19.1 %all_to_all.22 = bf16[4,40,640]{2,1,0:T(8,128)(2,1)S(1)} all-to-all(bf16[4,40,640]{2,1,0:T(8,128)(2,1)S(1)} %broadcast_in_dim.6), channel_id=1, replica_groups={{0,64,128,192},{16,80,144,208},{32,96,160,224},{48,112,176,240},{256,32..., dimensions={0} | all-to-all | bytes 409600 | tf_op jit(solution)/shard_map/middle_gather/all_to_all | solution.py:123
  103.7 1.0 broadcast_in_dim.15
  104.7 3.9 %all-to-all-start.3 = ((bf16[4,160,640]{2,1,0:T(8,128)(2,1)}), bf16[4,160,640]{2,1,0:T(8,128)(2,1)S(1)}, u32[]{:S(2)}, u32[]{:S(2)}) async-start(bf16[4,160,640]{2,1,0:T(8,128)(2,1)} %broadcast_in_dim.15), calls=%async_computation.3 | async-start | bytes 1638400 | tf_op jit(solution)/shard_map/near_gather/all_to_all | solution.py:123
  108.6 10.5 %all-to-all-done.3 = bf16[4,160,640]{2,1,0:T(8,128)(2,1)S(1)} async-done(((bf16[4,160,640]{2,1,0:T(8,128)(2,1)}), bf16[4,160,640]{2,1,0:T(8,128)(2,1)S(1)}, u32[]{:S(2)}, u32[]{:S(2)}) %all-to-all-start.3) | async-done | bytes 819232 | tf_op jit(solution)/shard_map/near_gather/all_to_all | solution.py:123
  119.1 5.7 %precondition.1 = f32[10,1,640]{2,1,0:T(1,128)} custom-call(s32[1]{0:T(128)} %bitcast.start_ref, bf16[640,640]{1,0:T(8,128)(2,1)S(1)} %bitcast.9), custom_call_target="tpu_custom_call" | custom-call | flops 3145728000 | bytes 819200 | tf_op jit(solution)/shard_map/precondition/pallas_call | solution.py:83
  (3 shorter events, 0.1 us)
Async XLA Ops:
  0.0 1.5 %copy-start = (bf16[1536,640]{1,0:T(8,128)(2,1)S(1)}, bf16[1536,640]{1,0:T(8,128)(2,1)}, u32[]{:S(2)}) copy-start(bf16[1536,640]{1,0:T(8,128)(2,1)} %param.2) | copy-start | bytes 5898244
  104.7 14.4 %all-to-all-start.3 = ((bf16[4,160,640]{2,1,0:T(8,128)(2,1)}), bf16[4,160,640]{2,1,0:T(8,128)(2,1)S(1)}, u32[]{:S(2)}, u32[]{:S(2)}) async-start(bf16[4,160,640]{2,1,0:T(8,128)(2,1)} %broadcast_in_dim.15), calls=%async_computation.3 | async-start | bytes 1638400 | tf_op jit(solution)/shard_map/near_gather/all_to_all | solution.py:123

commit v3 on v2

--- a/solution.py
+++ b/solution.py
@@ -28,7 +28,7 @@
 
 
 def precondition_kernel(
-    start_ref, g_ref, out_ref, stat, one, two, two_wide, three, mixed, base, wide, narrow, direction
+    g_ref, out_ref, stat, one, two, two_wide, three, mixed, base, wide, narrow, direction
 ):
     q = root_coefficients()
     extent = g_ref.shape[0]
@@ -71,12 +71,13 @@
         direction[rows, :] = part
         gradient_norm += folded(widened * widened)
         direction_norm += folded(part * part)
+    start = lax.axis_index("dp") * out_ref.shape[0]
     scale = jnp.sqrt(jnp.sum(gradient_norm) / (jnp.sum(direction_norm) + tiny_shift))
     for i in range(out_ref.shape[0]):
-        out_ref[i] = direction[pl.ds(start_ref[0] + i, 1), :] * scale
+        out_ref[i] = direction[pl.ds(start + i, 1), :] * scale
 
 
-def precondition(gradient, start, slab_rows):
+def precondition(gradient, slab_rows):
     extent = gradient.shape[0]
     square = (extent, extent)
     f32, bf16 = pltpu.VMEM(square, jnp.float32), pltpu.VMEM(square, jnp.bfloat16)
@@ -84,7 +85,6 @@
         precondition_kernel,
         out_shape=jax.ShapeDtypeStruct((slab_rows, 1, extent), jnp.float32),
         in_specs=[
-            pl.BlockSpec(memory_space=pltpu.SMEM),
             pl.BlockSpec(memory_space=pltpu.VMEM),
         ],
         out_specs=pl.BlockSpec(memory_space=pltpu.VMEM),
@@ -93,7 +93,7 @@
         cost_estimate=pl.CostEstimate(
             flops=12 * extent**3, bytes_accessed=2 * extent * extent, transcendentals=2
         ),
-    )(start, gradient)
+    )(gradient)
 
 
 def stage_groups():
@@ -134,7 +134,6 @@
 
 def per_device(activations, cotangent):
     dp_count = lax.axis_size("dp")
-    dp_index = lax.axis_index("dp")
     extent = cotangent.shape[1]
     slab_rows = extent // dp_count
     scaling = 1.0 / math.sqrt(activations.shape[0] * dp_count)
@@ -155,8 +154,7 @@
     with jax.named_scope("near_gather"):
         gradient = spread(part, near).reshape(extent, extent)
     with jax.named_scope("precondition"):
-        start = jnp.reshape(dp_index * slab_rows, (1,)).astype(jnp.int32)
-        return jnp.transpose(precondition(gradient, start, slab_rows), (1, 0, 2))
+        return jnp.transpose(precondition(gradient, slab_rows), (1, 0, 2))
 
 
 def solution(mesh):

time: 125 us -> 123 us (0.984)
  blocking collectives: 98.7 us -> 112 us
  waiting for transfers between devices: 10.5 us -> 0 us
  starting transfers between devices: 3.94 us -> 0 us
    all_to_all x3 -> x4, blocking collectives: 64.7 us -> 78.1 us  [exchange(): return lax.all_to_all(parts, axes, 0, 0, axis_index_groups=groups)]
    all_to_all x1 -> x0, waiting for transfers between devices: 10.5 us -> none  [exchange(): return lax.all_to_all(parts, axes, 0, 0, axis_index_groups=groups)]
    all_to_all x1 -> x0, starting transfers between devices: 3.94 us -> none  [exchange(): return lax.all_to_all(parts, axes, 0, 0, axis_index_groups=groups)]
  transfers between devices with their start and end apart: 1 -> 0, of which waited for: 1 -> 0; matrix products, arithmetic and copies ran while one was open for 0% -> 0% of each run, Pallas kernels for 0% -> 0%
where the time goes in v3:
time: 123 us
  blocking collectives  112 us (91%)
  Pallas kernels  5.67 us (5%)
  matrix products  3.28 us (3%)
  local copies, waits for them, and re-layouts  1.63 us (1%)
    all_to_all x4, blocking collectives, exchange(): return lax.all_to_all(parts, axes, 0, 0, axis_index_groups=groups)  78.1 us
    all_gather x1, blocking collectives, per_device(): part = summed(lax.all_gather(part, axes, axis_index_groups=far))  34 us
    pallas_call x1, Pallas kernels, precondition(): pl.pallas_call(precondition_kernel, out_shape=jax.ShapeDtypeStruct((slab_...  5.67 us
    dot_general x1, matrix products, per_device(): lax.dot_general(activations, cotangent, (((0,), (0,)), ((), ())), preferr...  3.28 us

profile of v3, /device:TPU:1, one launch (start us, length us, event | category | flops | bytes accessed | tf_op | source)
XLA Modules:
  0.0 122.8 jit_solution(11730434859547141825)
XLA Ops:
  0.0 0.0 copy-start
  0.0 1.5 %copy-done = bf16[1536,640]{1,0:T(8,128)(2,1)S(1)} copy-done((bf16[1536,640]{1,0:T(8,128)(2,1)S(1)}, bf16[1536,640]{1,0:T(8,128)(2,1)}, u32[]{:S(2)}) %copy-start) | copy-done | bytes 1966104
  1.5 3.3 %multiply_convert_fusion = bf16[640,640]{1,0:T(8,128)(2,1)S(1)} fusion(bf16[1536,640]{1,0:T(8,128)(2,1)S(1)} %copy-done, bf16[1536,640]{1,0:T(8,128)(2,1)} %param.3), kind=kOutput, calls=%fused_computation | convolution fusion | flops 1259110400 | bytes 4751360 | tf_op jit(solution)/shard_map/product/dot_general | solution.py:142
  4.8 28.4 %all_to_all.20 = bf16[4,160,640]{2,1,0:T(8,128)(2,1)S(1)} all-to-all(bf16[4,160,640]{2,1,0:T(8,128)(2,1)S(1)} %bitcast.10), channel_id=1, replica_groups={{0,16,32,48},{64,80,96,112},{128,144,160,176},{192,208,224,240},{256,27..., dimensions={0} | all-to-all | bytes 1638400 | tf_op jit(solution)/shard_map/near_sum/all_to_all | solution.py:123
  33.2 0.1 reduce_sum.36
  33.4 17.2 %all_to_all.21 = bf16[4,40,640]{2,1,0:T(8,128)(2,1)S(1)} all-to-all(bf16[4,40,640]{2,1,0:T(8,128)(2,1)S(1)} %bitcast.9), channel_id=1, replica_groups={{0,64,128,192},{16,80,144,208},{32,96,160,224},{48,112,176,240},{256,32..., dimensions={0} | all-to-all | bytes 409600 | tf_op jit(solution)/shard_map/middle_sum/all_to_all | solution.py:123
  50.6 34.0 %all-gather = bf16[160,640]{1,0:T(8,128)(2,1)S(1)} all-gather(bf16[40,640]{1,0:T(8,128)(2,1)S(1)} %reduce_sum.37), channel_id=2, replica_groups={{0,256,512,768},{16,272,528,784},{32,288,544,800},{48,304,560,816},{64,..., dimensions={0}, use_global_device_ids=true | all-gather | bytes 256000 | tf_op jit(solution)/shard_map/far_sum/all_gather | solution.py:151
  84.6 19.1 %all_to_all.22 = bf16[4,40,640]{2,1,0:T(8,128)(2,1)S(1)} all-to-all(bf16[4,40,640]{2,1,0:T(8,128)(2,1)S(1)} %broadcast_in_dim.6), channel_id=1, replica_groups={{0,64,128,192},{16,80,144,208},{32,96,160,224},{48,112,176,240},{256,32..., dimensions={0} | all-to-all | bytes 409600 | tf_op jit(solution)/shard_map/middle_gather/all_to_all | solution.py:123
  103.7 0.1 broadcast_in_dim.15
  103.8 13.3 %all_to_all.23 = bf16[4,160,640]{2,1,0:T(8,128)(2,1)S(1)} all-to-all(bf16[4,160,640]{2,1,0:T(8,128)(2,1)S(1)} %broadcast_in_dim.15), channel_id=1, replica_groups={{0,16,32,48},{64,80,96,112},{128,144,160,176},{192,208,224,240},{256,27..., dimensions={0} | all-to-all | bytes 1638400 | tf_op jit(solution)/shard_map/near_gather/all_to_all | solution.py:123
  117.2 5.7 %precondition.1 = f32[10,1,640]{2,1,0:T(1,128)} custom-call(bf16[640,640]{1,0:T(8,128)(2,1)S(1)} %bitcast.8), custom_call_target="tpu_custom_call" | custom-call | flops 3145728000 | bytes 819200 | tf_op jit(solution)/shard_map/precondition/pallas_call | solution.py:84
  (3 shorter events, 0.1 us)
Async XLA Ops:
  0.0 1.5 %copy-start = (bf16[1536,640]{1,0:T(8,128)(2,1)S(1)}, bf16[1536,640]{1,0:T(8,128)(2,1)}, u32[]{:S(2)}) copy-start(bf16[1536,640]{1,0:T(8,128)(2,1)} %param.2) | copy-start | bytes 5898244

commit v4 on v3

--- a/solution.py
+++ b/solution.py
@@ -1,3 +1,4 @@
+import functools
 import math
 
 import jax
@@ -12,8 +13,7 @@
 tiny_shift = 1e-12
 chunk = 640
 axes = ("dp", "mp", "blk")
-core_shift = 9
-stage_bits = (((0, 1), (2, 3), (4, 5)), ((0, 1), (2, 3), (4, 5)))
+core_shifts = (30, 27)
 
 
 def root_coefficients():
@@ -96,27 +96,39 @@
     )(gradient)
 
 
-def stage_groups():
+def flat_index(virtual, mp, blk):
     count, n_mp, n_blk = (lax.axis_size(axis) for axis in axes)
-    rings = count // 2
+    place = (virtual // 2 + core_shifts[blk % 2]) % (count // 2) * 2 + virtual % 2
+    return (place * n_mp + mp) * n_blk + blk
 
-    def placed(stage):
-        groups = []
-        for mp in range(n_mp):
-            for blk in range(n_blk):
-                core = blk % 2
-                low, high = (1 << bit for bit in stage_bits[core][stage])
-                for base in range(count):
-                    if base & (low | high):
-                        continue
-                    members = [base, base | low, base | high, base | low | high]
-                    groups.append([
-                        (((v // 2 + core_shift * core) % rings * 2 + v % 2) * n_mp + mp) * n_blk + blk
-                        for v in members
-                    ])
-        return groups
 
-    return [placed(stage) for stage in range(3)]
+def columns():
+    return [(mp, blk) for mp in range(lax.axis_size("mp")) for blk in range(lax.axis_size("blk"))]
+
+
+def stage_groups(low, high):
+    return [
+        [flat_index(base | member, mp, blk) for member in (0, low, high, low | high)]
+        for mp, blk in columns()
+        for base in range(lax.axis_size("dp"))
+        if not base & (low | high)
+    ]
+
+
+def far_sum(part):
+    count = lax.axis_size("dp")
+    links = [
+        [(flat_index(source, mp, blk), flat_index(source % 16, mp, blk)) for mp, blk in columns() for source in range(16 * run, 16 * run + 16)]
+        for run in range(1, count // 16)
+    ]
+    total = part.astype(jnp.float32)
+    for received in [lax.ppermute(part, axes, link) for link in links]:
+        total += received.astype(jnp.float32)
+    total = total.astype(jnp.bfloat16)
+    returned = [lax.ppermute(total, axes, [(b, a) for a, b in link]) for link in links]
+    shift = jnp.where(lax.axis_index("blk") % 2 == 0, core_shifts[0], core_shifts[1])
+    first = (lax.axis_index("dp") // 2 - shift) % (count // 2) < 8
+    return jnp.where(first, total, functools.reduce(jnp.add, returned))
 
 
 def exchange(parts, groups):
@@ -137,7 +149,7 @@
     extent = cotangent.shape[1]
     slab_rows = extent // dp_count
     scaling = 1.0 / math.sqrt(activations.shape[0] * dp_count)
-    near, middle, far = stage_groups()
+    near, middle = stage_groups(1, 2), stage_groups(4, 8)
     with jax.named_scope("product"):
         product = lax.dot_general(
             activations, cotangent, (((0,), (0,)), ((), ())), preferred_element_type=jnp.float32
@@ -148,7 +160,7 @@
     with jax.named_scope("middle_sum"):
         part = summed(exchange(part.reshape(4, extent // 16, extent), middle))
     with jax.named_scope("far_sum"):
-        part = summed(lax.all_gather(part, axes, axis_index_groups=far))
+        part = far_sum(part)
     with jax.named_scope("middle_gather"):
         part = spread(part, middle).reshape(extent // 4, extent)
     with jax.named_scope("near_gather"):

time: 123 us -> 122 us (level)
  blocking collectives: 112 us -> 81.1 us
  waiting for transfers between devices: 0 us -> 21.7 us
  starting transfers between devices: 0 us -> 7.75 us
    all_gather x1 -> x0, blocking collectives: 34 us -> none  [per_device(): part = summed(lax.all_gather(part, axes, axis_index_groups=far))]
    ppermute x0 -> x6, waiting for transfers between devices: none -> 21.7 us  [the longest x3 20.6 us: far_sum(): lax.ppermute(part, axes, link)]
    ppermute x0 -> x6, starting transfers between devices: none -> 7.75 us  [the longest x3 3.88 us: far_sum(): lax.ppermute(total, axes, [(b, a) for a, b in link])]
    all_to_all x4, blocking collectives: 78.1 us -> 81.1 us  [exchange(): return lax.all_to_all(parts, axes, 0, 0, axis_index_groups=groups)]
  transfers between devices with their start and end apart: 0 -> 6, of which waited for: 0 -> 3; matrix products, arithmetic and copies ran while one was open for 0% -> 0% of each run, Pallas kernels for 0% -> 0%
where the time goes in v4:
time: 122 us
  blocking collectives  81.1 us (66%)
  waiting for transfers between devices  21.7 us (18%)
  starting transfers between devices  7.75 us (6%)
  Pallas kernels  5.66 us (5%)
  matrix products  3.28 us (3%)
  local copies, waits for them, and re-layouts  1.63 us (1%)
    all_to_all x4, blocking collectives, exchange(): return lax.all_to_all(parts, axes, 0, 0, axis_index_groups=groups)  81.1 us
    ppermute x3, waiting for transfers between devices, far_sum(): lax.ppermute(part, axes, link)  20.6 us
    pallas_call x1, Pallas kernels, precondition(): pl.pallas_call(precondition_kernel, out_shape=jax.ShapeDtypeStruct((slab_...  5.66 us
    ppermute x3, starting transfers between devices, far_sum(): lax.ppermute(total, axes, [(b, a) for a, b in link])  3.88 us
    ppermute x3, starting transfers between devices, far_sum(): lax.ppermute(part, axes, link)  3.88 us
    dot_general x1, matrix products, per_device(): lax.dot_general(activations, cotangent, (((0,), (0,)), ((), ())), preferr...  3.28 us
  transfers between devices with their start and end apart: 6, of which 3 were waited for; matrix products, arithmetic and copies ran while one was open for 0% of the time, Pallas kernels for 0%

profile of v4, /device:TPU:1, one launch (start us, length us, event | category | flops | bytes accessed | tf_op | source)
XLA Modules:
  0.0 121.5 jit_solution(8522318328809229242)
XLA Ops:
  0.0 0.0 copy-start
  0.0 1.5 %copy-done = bf16[1536,640]{1,0:T(8,128)(2,1)S(1)} copy-done((bf16[1536,640]{1,0:T(8,128)(2,1)S(1)}, bf16[1536,640]{1,0:T(8,128)(2,1)}, u32[]{:S(2)}) %copy-start) | copy-done | bytes 1966104
  1.5 3.3 %multiply_convert_fusion = bf16[640,640]{1,0:T(8,128)(2,1)S(1)} fusion(bf16[1536,640]{1,0:T(8,128)(2,1)S(1)} %copy-done, bf16[1536,640]{1,0:T(8,128)(2,1)} %param.3), kind=kOutput, calls=%fused_computation | convolution fusion | flops 1259110400 | bytes 4751360 | tf_op jit(solution)/shard_map/product/dot_general | solution.py:154
  4.8 28.4 %all_to_all.20 = bf16[4,160,640]{2,1,0:T(8,128)(2,1)S(1)} all-to-all(bf16[4,160,640]{2,1,0:T(8,128)(2,1)S(1)} %bitcast.9), channel_id=1, replica_groups={{960,976,992,1008},{0,16,32,48},{64,80,96,112},{128,144,160,176},{192,2..., dimensions={0} | all-to-all | bytes 1638400 | tf_op jit(solution)/shard_map/near_sum/all_to_all | solution.py:135
  33.2 0.1 reduce_sum.24
  33.4 14.4 %all_to_all.21 = bf16[4,40,640]{2,1,0:T(8,128)(2,1)S(1)} all-to-all(bf16[4,40,640]{2,1,0:T(8,128)(2,1)S(1)} %bitcast.8), channel_id=1, replica_groups={{960,0,64,128},{976,16,80,144},{992,32,96,160},{1008,48,112,176},{192,2..., dimensions={0} | all-to-all | bytes 409600 | tf_op jit(solution)/shard_map/middle_sum/all_to_all | solution.py:135
  47.8 1.3 %collective-permute-start.2 = (bf16[40,640]{1,0:T(8,128)(2,1)S(1)}, bf16[40,640]{1,0:T(8,128)(2,1)S(1)}, u32[]{:S(2)}, u32[]{:S(2)}) collective-permute-start(bf16[40,640]{1,0:T(8,128)(2,1)S(1)} %reduce_sum.25), channel_id=1, source_target_pairs={{704,960},{720,976},{736,992},{752,1008},{768,0},{784,16},{800,32}... | collective-permute-start | bytes 153608 | tf_op jit(solution)/shard_map/far_sum/ppermute | solution.py:125
  49.1 1.3 %collective-permute-start.1 = (bf16[40,640]{1,0:T(8,128)(2,1)S(1)}, bf16[40,640]{1,0:T(8,128)(2,1)S(1)}, u32[]{:S(2)}, u32[]{:S(2)}) collective-permute-start(bf16[40,640]{1,0:T(8,128)(2,1)S(1)} %reduce_sum.25), channel_id=1, source_target_pairs={{448,960},{464,976},{480,992},{496,1008},{512,0},{528,16},{544,32}... | collective-permute-start | bytes 153608 | tf_op jit(solution)/shard_map/far_sum/ppermute | solution.py:125
  50.4 1.3 %collective-permute-start = (bf16[40,640]{1,0:T(8,128)(2,1)S(1)}, bf16[40,640]{1,0:T(8,128)(2,1)S(1)}, u32[]{:S(2)}, u32[]{:S(2)}) collective-permute-start(bf16[40,640]{1,0:T(8,128)(2,1)S(1)} %reduce_sum.25), channel_id=1, source_target_pairs={{192,960},{208,976},{224,992},{240,1008},{256,0},{272,16},{288,32}... | collective-permute-start | bytes 153608 | tf_op jit(solution)/shard_map/far_sum/ppermute | solution.py:125
  51.7 9.8 %collective-permute-done.2 = bf16[40,640]{1,0:T(8,128)(2,1)S(1)} collective-permute-done((bf16[40,640]{1,0:T(8,128)(2,1)S(1)}, bf16[40,640]{1,0:T(8,128)(2,1)S(1)}, u32[]{:S(2)}, u32[]{:S(2)}) %collective-permute-start.2) | collective-permute-done | bytes 51232 | tf_op jit(solution)/shard_map/far_sum/ppermute | solution.py:125
  61.5 10.8 %collective-permute-done.1 = bf16[40,640]{1,0:T(8,128)(2,1)S(1)} collective-permute-done((bf16[40,640]{1,0:T(8,128)(2,1)S(1)}, bf16[40,640]{1,0:T(8,128)(2,1)S(1)}, u32[]{:S(2)}, u32[]{:S(2)}) %collective-permute-start.1) | collective-permute-done | bytes 51232 | tf_op jit(solution)/shard_map/far_sum/ppermute | solution.py:125
  72.3 0.0 collective-permute-done
  72.3 1.3 %collective-permute-start.5 = (bf16[40,640]{1,0:T(8,128)(2,1)S(1)}, bf16[40,640]{1,0:T(8,128)(2,1)S(1)}, u32[]{:S(2)}, u32[]{:S(2)}) collective-permute-start(bf16[40,640]{1,0:T(8,128)(2,1)S(1)} %add_convert_fusion), channel_id=1, source_target_pairs={{960,704},{976,720},{992,736},{1008,752},{0,768},{16,784},{32,800}... | collective-permute-start | bytes 153608 | tf_op jit(solution)/shard_map/far_sum/ppermute | solution.py:128
  73.6 1.3 %collective-permute-start.3 = (bf16[40,640]{1,0:T(8,128)(2,1)S(1)}, bf16[40,640]{1,0:T(8,128)(2,1)S(1)}, u32[]{:S(2)}, u32[]{:S(2)}) collective-permute-start(bf16[40,640]{1,0:T(8,128)(2,1)S(1)} %add_convert_fusion), channel_id=1, source_target_pairs={{960,192},{976,208},{992,224},{1008,240},{0,256},{16,272},{32,288}... | collective-permute-start | bytes 153608 | tf_op jit(solution)/shard_map/far_sum/ppermute | solution.py:128
  74.9 1.3 %collective-permute-start.4 = (bf16[40,640]{1,0:T(8,128)(2,1)S(1)}, bf16[40,640]{1,0:T(8,128)(2,1)S(1)}, u32[]{:S(2)}, u32[]{:S(2)}) collective-permute-start(bf16[40,640]{1,0:T(8,128)(2,1)S(1)} %add_convert_fusion), channel_id=1, source_target_pairs={{960,448},{976,464},{992,480},{1008,496},{0,512},{16,528},{32,544}... | collective-permute-start | bytes 153608 | tf_op jit(solution)/shard_map/far_sum/ppermute | solution.py:128
  76.3 0.0 collective-permute-done.5
  76.3 0.0 collective-permute-done.3
  76.3 1.1 collective-permute-done.4
  77.5 17.8 %all_to_all.22 = bf16[4,40,640]{2,1,0:T(8,128)(2,1)S(1)} all-to-all(bf16[4,40,640]{2,1,0:T(8,128)(2,1)S(1)} %broadcast_in_dim.6), channel_id=1, replica_groups={{960,0,64,128},{976,16,80,144},{992,32,96,160},{1008,48,112,176},{192,2..., dimensions={0} | all-to-all | bytes 409600 | tf_op jit(solution)/shard_map/middle_gather/all_to_all | solution.py:135
  95.3 0.1 broadcast_in_dim.15
  95.3 20.6 %all_to_all.23 = bf16[4,160,640]{2,1,0:T(8,128)(2,1)S(1)} all-to-all(bf16[4,160,640]{2,1,0:T(8,128)(2,1)S(1)} %broadcast_in_dim.15), channel_id=1, replica_groups={{960,976,992,1008},{0,16,32,48},{64,80,96,112},{128,144,160,176},{192,2..., dimensions={0} | all-to-all | bytes 1638400 | tf_op jit(solution)/shard_map/near_gather/all_to_all | solution.py:135
  115.9 5.7 %precondition.1 = f32[10,1,640]{2,1,0:T(1,128)} custom-call(bf16[640,640]{1,0:T(8,128)(2,1)S(1)} %bitcast.7), custom_call_target="tpu_custom_call" | custom-call | flops 3145728000 | bytes 819200 | tf_op jit(solution)/shard_map/precondition/pallas_call | solution.py:84
  (4 shorter events, 0.1 us)
Async XLA Ops:
  0.0 1.5 %copy-start = (bf16[1536,640]{1,0:T(8,128)(2,1)S(1)}, bf16[1536,640]{1,0:T(8,128)(2,1)}, u32[]{:S(2)}) copy-start(bf16[1536,640]{1,0:T(8,128)(2,1)} %param.2) | copy-start | bytes 5898244
  47.8 13.7 %collective-permute-start.2 = (bf16[40,640]{1,0:T(8,128)(2,1)S(1)}, bf16[40,640]{1,0:T(8,128)(2,1)S(1)}, u32[]{:S(2)}, u32[]{:S(2)}) collective-permute-start(bf16[40,640]{1,0:T(8,128)(2,1)S(1)} %reduce_sum.25), channel_id=1, source_target_pairs={{704,960},{720,976},{736,992},{752,1008},{768,0},{784,16},{800,32}... | collective-permute-start | bytes 153608 | tf_op jit(solution)/shard_map/far_sum/ppermute | solution.py:125
  49.1 23.2 %collective-permute-start.1 = (bf16[40,640]{1,0:T(8,128)(2,1)S(1)}, bf16[40,640]{1,0:T(8,128)(2,1)S(1)}, u32[]{:S(2)}, u32[]{:S(2)}) collective-permute-start(bf16[40,640]{1,0:T(8,128)(2,1)S(1)} %reduce_sum.25), channel_id=1, source_target_pairs={{448,960},{464,976},{480,992},{496,1008},{512,0},{528,16},{544,32}... | collective-permute-start | bytes 153608 | tf_op jit(solution)/shard_map/far_sum/ppermute | solution.py:125
  50.4 21.9 %collective-permute-start = (bf16[40,640]{1,0:T(8,128)(2,1)S(1)}, bf16[40,640]{1,0:T(8,128)(2,1)S(1)}, u32[]{:S(2)}, u32[]{:S(2)}) collective-permute-start(bf16[40,640]{1,0:T(8,128)(2,1)S(1)} %reduce_sum.25), channel_id=1, source_target_pairs={{192,960},{208,976},{224,992},{240,1008},{256,0},{272,16},{288,32}... | collective-permute-start | bytes 153608 | tf_op jit(solution)/shard_map/far_sum/ppermute | solution.py:125
  72.3 3.9 %collective-permute-start.5 = (bf16[40,640]{1,0:T(8,128)(2,1)S(1)}, bf16[40,640]{1,0:T(8,128)(2,1)S(1)}, u32[]{:S(2)}, u32[]{:S(2)}) collective-permute-start(bf16[40,640]{1,0:T(8,128)(2,1)S(1)} %add_convert_fusion), channel_id=1, source_target_pairs={{960,704},{976,720},{992,736},{1008,752},{0,768},{16,784},{32,800}... | collective-permute-start | bytes 153608 | tf_op jit(solution)/shard_map/far_sum/ppermute | solution.py:128
  73.6 2.7 %collective-permute-start.3 = (bf16[40,640]{1,0:T(8,128)(2,1)S(1)}, bf16[40,640]{1,0:T(8,128)(2,1)S(1)}, u32[]{:S(2)}, u32[]{:S(2)}) collective-permute-start(bf16[40,640]{1,0:T(8,128)(2,1)S(1)} %add_convert_fusion), channel_id=1, source_target_pairs={{960,192},{976,208},{992,224},{1008,240},{0,256},{16,272},{32,288}... | collective-permute-start | bytes 153608 | tf_op jit(solution)/shard_map/far_sum/ppermute | solution.py:128
  74.9 2.5 %collective-permute-start.4 = (bf16[40,640]{1,0:T(8,128)(2,1)S(1)}, bf16[40,640]{1,0:T(8,128)(2,1)S(1)}, u32[]{:S(2)}, u32[]{:S(2)}) collective-permute-start(bf16[40,640]{1,0:T(8,128)(2,1)S(1)} %add_convert_fusion), channel_id=1, source_target_pairs={{960,448},{976,464},{992,480},{1008,496},{0,512},{16,528},{32,544}... | collective-permute-start | bytes 153608 | tf_op jit(solution)/shard_map/far_sum/ppermute | solution.py:128

commit v5 on v4

--- a/solution.py
+++ b/solution.py
@@ -13,7 +13,7 @@
 tiny_shift = 1e-12
 chunk = 640
 axes = ("dp", "mp", "blk")
-core_shifts = (30, 27)
+core_shifts = (0, 27)
 
 
 def root_coefficients():

time: 122 us -> 119 us (0.975)
  the two profiles are of different devices: /device:TPU:1 before, /device:TPU:8 now
where the time goes in v5:
time: 119 us
  blocking collectives  73.7 us (62%)
  waiting for transfers between devices  26.5 us (22%)
  starting transfers between devices  7.75 us (7%)
  Pallas kernels  5.67 us (5%)
  matrix products  3.28 us (3%)
  local copies, waits for them, and re-layouts  1.63 us (1%)
    all_to_all x4, blocking collectives, exchange(): return lax.all_to_all(parts, axes, 0, 0, axis_index_groups=groups)  73.7 us
    ppermute x3, waiting for transfers between devices, far_sum(): lax.ppermute(part, axes, link)  21.8 us
    pallas_call x1, Pallas kernels, precondition(): pl.pallas_call(precondition_kernel, out_shape=jax.ShapeDtypeStruct((slab_...  5.67 us
    ppermute x3, waiting for transfers between devices, far_sum(): lax.ppermute(total, axes, [(b, a) for a, b in link])  4.74 us
    ppermute x3, starting transfers between devices, far_sum(): lax.ppermute(total, axes, [(b, a) for a, b in link])  3.88 us
    ppermute x3, starting transfers between devices, far_sum(): lax.ppermute(part, axes, link)  3.88 us
    dot_general x1, matrix products, per_device(): lax.dot_general(activations, cotangent, (((0,), (0,)), ((), ())), preferr...  3.28 us
  transfers between devices with their start and end apart: 6, of which 4 were waited for; matrix products, arithmetic and copies ran while one was open for 0% of the time, Pallas kernels for 0%

profile of v5, /device:TPU:8, one launch (start us, length us, event | category | flops | bytes accessed | tf_op | source)
XLA Modules:
  0.0 118.9 jit_solution(10615063426726669008)
XLA Ops:
  0.0 0.0 copy-start
  0.0 1.5 %copy-done = bf16[1536,640]{1,0:T(8,128)(2,1)S(1)} copy-done((bf16[1536,640]{1,0:T(8,128)(2,1)S(1)}, bf16[1536,640]{1,0:T(8,128)(2,1)}, u32[]{:S(2)}) %copy-start) | copy-done | bytes 1966104
  1.5 3.3 %multiply_convert_fusion = bf16[640,640]{1,0:T(8,128)(2,1)S(1)} fusion(bf16[1536,640]{1,0:T(8,128)(2,1)S(1)} %copy-done, bf16[1536,640]{1,0:T(8,128)(2,1)} %param.3), kind=kOutput, calls=%fused_computation | convolution fusion | flops 1259110400 | bytes 4751360 | tf_op jit(solution)/shard_map/product/dot_general | solution.py:154
  4.8 23.7 %all_to_all.20 = bf16[4,160,640]{2,1,0:T(8,128)(2,1)S(1)} all-to-all(bf16[4,160,640]{2,1,0:T(8,128)(2,1)S(1)} %bitcast.9), channel_id=1, replica_groups={{0,16,32,48},{64,80,96,112},{128,144,160,176},{192,208,224,240},{256,27..., dimensions={0} | all-to-all | bytes 1638400 | tf_op jit(solution)/shard_map/near_sum/all_to_all | solution.py:135
  28.6 0.1 reduce_sum.24
  28.7 16.5 %all_to_all.21 = bf16[4,40,640]{2,1,0:T(8,128)(2,1)S(1)} all-to-all(bf16[4,40,640]{2,1,0:T(8,128)(2,1)S(1)} %bitcast.8), channel_id=1, replica_groups={{0,64,128,192},{16,80,144,208},{32,96,160,224},{48,112,176,240},{256,32..., dimensions={0} | all-to-all | bytes 409600 | tf_op jit(solution)/shard_map/middle_sum/all_to_all | solution.py:135
  45.2 1.3 %collective-permute-start.2 = (bf16[40,640]{1,0:T(8,128)(2,1)S(1)}, bf16[40,640]{1,0:T(8,128)(2,1)S(1)}, u32[]{:S(2)}, u32[]{:S(2)}) collective-permute-start(bf16[40,640]{1,0:T(8,128)(2,1)S(1)} %reduce_sum.25), channel_id=1, source_target_pairs={{768,0},{784,16},{800,32},{816,48},{832,64},{848,80},{864,96},{880... | collective-permute-start | bytes 153608 | tf_op jit(solution)/shard_map/far_sum/ppermute | solution.py:125
  46.5 1.3 %collective-permute-start.1 = (bf16[40,640]{1,0:T(8,128)(2,1)S(1)}, bf16[40,640]{1,0:T(8,128)(2,1)S(1)}, u32[]{:S(2)}, u32[]{:S(2)}) collective-permute-start(bf16[40,640]{1,0:T(8,128)(2,1)S(1)} %reduce_sum.25), channel_id=1, source_target_pairs={{512,0},{528,16},{544,32},{560,48},{576,64},{592,80},{608,96},{624... | collective-permute-start | bytes 153608 | tf_op jit(solution)/shard_map/far_sum/ppermute | solution.py:125
  47.8 1.3 %collective-permute-start = (bf16[40,640]{1,0:T(8,128)(2,1)S(1)}, bf16[40,640]{1,0:T(8,128)(2,1)S(1)}, u32[]{:S(2)}, u32[]{:S(2)}) collective-permute-start(bf16[40,640]{1,0:T(8,128)(2,1)S(1)} %reduce_sum.25), channel_id=1, source_target_pairs={{256,0},{272,16},{288,32},{304,48},{320,64},{336,80},{352,96},{368... | collective-permute-start | bytes 153608 | tf_op jit(solution)/shard_map/far_sum/ppermute | solution.py:125
  49.1 12.2 %collective-permute-done.2 = bf16[40,640]{1,0:T(8,128)(2,1)S(1)} collective-permute-done((bf16[40,640]{1,0:T(8,128)(2,1)S(1)}, bf16[40,640]{1,0:T(8,128)(2,1)S(1)}, u32[]{:S(2)}, u32[]{:S(2)}) %collective-permute-start.2) | collective-permute-done | bytes 51232 | tf_op jit(solution)/shard_map/far_sum/ppermute | solution.py:125
  61.3 9.6 %collective-permute-done.1 = bf16[40,640]{1,0:T(8,128)(2,1)S(1)} collective-permute-done((bf16[40,640]{1,0:T(8,128)(2,1)S(1)}, bf16[40,640]{1,0:T(8,128)(2,1)S(1)}, u32[]{:S(2)}, u32[]{:S(2)}) %collective-permute-start.1) | collective-permute-done | bytes 51232 | tf_op jit(solution)/shard_map/far_sum/ppermute | solution.py:125
  70.9 0.0 collective-permute-done
  70.9 1.3 %collective-permute-start.5 = (bf16[40,640]{1,0:T(8,128)(2,1)S(1)}, bf16[40,640]{1,0:T(8,128)(2,1)S(1)}, u32[]{:S(2)}, u32[]{:S(2)}) collective-permute-start(bf16[40,640]{1,0:T(8,128)(2,1)S(1)} %add_convert_fusion), channel_id=1, source_target_pairs={{0,768},{16,784},{32,800},{48,816},{64,832},{80,848},{96,864},{112... | collective-permute-start | bytes 153608 | tf_op jit(solution)/shard_map/far_sum/ppermute | solution.py:128
  72.2 1.3 %collective-permute-start.3 = (bf16[40,640]{1,0:T(8,128)(2,1)S(1)}, bf16[40,640]{1,0:T(8,128)(2,1)S(1)}, u32[]{:S(2)}, u32[]{:S(2)}) collective-permute-start(bf16[40,640]{1,0:T(8,128)(2,1)S(1)} %add_convert_fusion), channel_id=1, source_target_pairs={{0,256},{16,272},{32,288},{48,304},{64,320},{80,336},{96,352},{112... | collective-permute-start | bytes 153608 | tf_op jit(solution)/shard_map/far_sum/ppermute | solution.py:128
  73.5 1.3 %collective-permute-start.4 = (bf16[40,640]{1,0:T(8,128)(2,1)S(1)}, bf16[40,640]{1,0:T(8,128)(2,1)S(1)}, u32[]{:S(2)}, u32[]{:S(2)}) collective-permute-start(bf16[40,640]{1,0:T(8,128)(2,1)S(1)} %add_convert_fusion), channel_id=1, source_target_pairs={{0,512},{16,528},{32,544},{48,560},{64,576},{80,592},{96,608},{112... | collective-permute-start | bytes 153608 | tf_op jit(solution)/shard_map/far_sum/ppermute | solution.py:128
  74.9 0.0 collective-permute-done.5
  74.9 4.2 %collective-permute-done.3 = bf16[40,640]{1,0:T(8,128)(2,1)S(1)} collective-permute-done((bf16[40,640]{1,0:T(8,128)(2,1)S(1)}, bf16[40,640]{1,0:T(8,128)(2,1)S(1)}, u32[]{:S(2)}, u32[]{:S(2)}) %collective-permute-start.3) | collective-permute-done | bytes 51232 | tf_op jit(solution)/shard_map/far_sum/ppermute | solution.py:128
  79.1 0.5 collective-permute-done.4
  79.7 18.8 %all_to_all.22 = bf16[4,40,640]{2,1,0:T(8,128)(2,1)S(1)} all-to-all(bf16[4,40,640]{2,1,0:T(8,128)(2,1)S(1)} %broadcast_in_dim.6), channel_id=1, replica_groups={{0,64,128,192},{16,80,144,208},{32,96,160,224},{48,112,176,240},{256,32..., dimensions={0} | all-to-all | bytes 409600 | tf_op jit(solution)/shard_map/middle_gather/all_to_all | solution.py:135
  98.4 0.1 broadcast_in_dim.15
  98.5 14.7 %all_to_all.23 = bf16[4,160,640]{2,1,0:T(8,128)(2,1)S(1)} all-to-all(bf16[4,160,640]{2,1,0:T(8,128)(2,1)S(1)} %broadcast_in_dim.15), channel_id=1, replica_groups={{0,16,32,48},{64,80,96,112},{128,144,160,176},{192,208,224,240},{256,27..., dimensions={0} | all-to-all | bytes 1638400 | tf_op jit(solution)/shard_map/near_gather/all_to_all | solution.py:135
  113.2 5.7 %precondition.1 = f32[10,1,640]{2,1,0:T(1,128)} custom-call(bf16[640,640]{1,0:T(8,128)(2,1)S(1)} %bitcast.7), custom_call_target="tpu_custom_call" | custom-call | flops 3145728000 | bytes 819200 | tf_op jit(solution)/shard_map/precondition/pallas_call | solution.py:84
  (4 shorter events, 0.1 us)
Async XLA Ops:
  0.0 1.5 %copy-start = (bf16[1536,640]{1,0:T(8,128)(2,1)S(1)}, bf16[1536,640]{1,0:T(8,128)(2,1)}, u32[]{:S(2)}) copy-start(bf16[1536,640]{1,0:T(8,128)(2,1)} %param.2) | copy-start | bytes 5898244
  45.2 16.1 %collective-permute-start.2 = (bf16[40,640]{1,0:T(8,128)(2,1)S(1)}, bf16[40,640]{1,0:T(8,128)(2,1)S(1)}, u32[]{:S(2)}, u32[]{:S(2)}) collective-permute-start(bf16[40,640]{1,0:T(8,128)(2,1)S(1)} %reduce_sum.25), channel_id=1, source_target_pairs={{768,0},{784,16},{800,32},{816,48},{832,64},{848,80},{864,96},{880... | collective-permute-start | bytes 153608 | tf_op jit(solution)/shard_map/far_sum/ppermute | solution.py:125
  46.5 24.4 %collective-permute-start.1 = (bf16[40,640]{1,0:T(8,128)(2,1)S(1)}, bf16[40,640]{1,0:T(8,128)(2,1)S(1)}, u32[]{:S(2)}, u32[]{:S(2)}) collective-permute-start(bf16[40,640]{1,0:T(8,128)(2,1)S(1)} %reduce_sum.25), channel_id=1, source_target_pairs={{512,0},{528,16},{544,32},{560,48},{576,64},{592,80},{608,96},{624... | collective-permute-start | bytes 153608 | tf_op jit(solution)/shard_map/far_sum/ppermute | solution.py:125
  47.8 23.1 %collective-permute-start = (bf16[40,640]{1,0:T(8,128)(2,1)S(1)}, bf16[40,640]{1,0:T(8,128)(2,1)S(1)}, u32[]{:S(2)}, u32[]{:S(2)}) collective-permute-start(bf16[40,640]{1,0:T(8,128)(2,1)S(1)} %reduce_sum.25), channel_id=1, source_target_pairs={{256,0},{272,16},{288,32},{304,48},{320,64},{336,80},{352,96},{368... | collective-permute-start | bytes 153608 | tf_op jit(solution)/shard_map/far_sum/ppermute | solution.py:125
  70.9 3.9 %collective-permute-start.5 = (bf16[40,640]{1,0:T(8,128)(2,1)S(1)}, bf16[40,640]{1,0:T(8,128)(2,1)S(1)}, u32[]{:S(2)}, u32[]{:S(2)}) collective-permute-start(bf16[40,640]{1,0:T(8,128)(2,1)S(1)} %add_convert_fusion), channel_id=1, source_target_pairs={{0,768},{16,784},{32,800},{48,816},{64,832},{80,848},{96,864},{112... | collective-permute-start | bytes 153608 | tf_op jit(solution)/shard_map/far_sum/ppermute | solution.py:128
  72.2 6.9 %collective-permute-start.3 = (bf16[40,640]{1,0:T(8,128)(2,1)S(1)}, bf16[40,640]{1,0:T(8,128)(2,1)S(1)}, u32[]{:S(2)}, u32[]{:S(2)}) collective-permute-start(bf16[40,640]{1,0:T(8,128)(2,1)S(1)} %add_convert_fusion), channel_id=1, source_target_pairs={{0,256},{16,272},{32,288},{48,304},{64,320},{80,336},{96,352},{112... | collective-permute-start | bytes 153608 | tf_op jit(solution)/shard_map/far_sum/ppermute | solution.py:128
  73.5 6.1 %collective-permute-start.4 = (bf16[40,640]{1,0:T(8,128)(2,1)S(1)}, bf16[40,640]{1,0:T(8,128)(2,1)S(1)}, u32[]{:S(2)}, u32[]{:S(2)}) collective-permute-start(bf16[40,640]{1,0:T(8,128)(2,1)S(1)} %add_convert_fusion), channel_id=1, source_target_pairs={{0,512},{16,528},{32,544},{48,560},{64,576},{80,592},{96,608},{112... | collective-permute-start | bytes 153608 | tf_op jit(solution)/shard_map/far_sum/ppermute | solution.py:128

commit v6 on v5

--- a/solution.py
+++ b/solution.py
@@ -119,7 +119,7 @@
     count = lax.axis_size("dp")
     links = [
         [(flat_index(source, mp, blk), flat_index(source % 16, mp, blk)) for mp, blk in columns() for source in range(16 * run, 16 * run + 16)]
-        for run in range(1, count // 16)
+        for run in (1, 3, 2)
     ]
     total = part.astype(jnp.float32)
     for received in [lax.ppermute(part, axes, link) for link in links]:

time: 119 us -> 119 us (level)
  the two profiles are of different devices: /device:TPU:8 before, /device:TPU:1 now
where the time goes in v6:
time: 119 us; the launch traced here: 118 us
  blocking collectives  71.7 us (60%)
  waiting for transfers between devices  27.7 us (23%)
  starting transfers between devices  8.16 us (7%)
  Pallas kernels  5.66 us (5%)
  matrix products  3.28 us (3%)
  local copies, waits for them, and re-layouts  1.63 us (1%)
    all_to_all x4, blocking collectives, exchange(): return lax.all_to_all(parts, axes, 0, 0, axis_index_groups=groups)  71.7 us
    ppermute x3, waiting for transfers between devices, far_sum(): lax.ppermute(part, axes, link)  19.4 us
    ppermute x3, waiting for transfers between devices, far_sum(): lax.ppermute(total, axes, [(b, a) for a, b in link])  8.31 us
    pallas_call x1, Pallas kernels, precondition(): pl.pallas_call(precondition_kernel, out_shape=jax.ShapeDtypeStruct((slab_...  5.66 us
    ppermute x3, starting transfers between devices, far_sum(): lax.ppermute(total, axes, [(b, a) for a, b in link])  4.29 us
    ppermute x3, starting transfers between devices, far_sum(): lax.ppermute(part, axes, link)  3.88 us
    dot_general x1, matrix products, per_device(): lax.dot_general(activations, cotangent, (((0,), (0,)), ((), ())), preferr...  3.28 us
  transfers between devices with their start and end apart: 6, of which 2 were waited for; matrix products, arithmetic and copies ran while one was open for 0% of the time, Pallas kernels for 0%

profile of v6, /device:TPU:1, one launch (start us, length us, event | category | flops | bytes accessed | tf_op | source)
XLA Modules:
  0.0 118.5 jit_solution(147169873856941256)
XLA Ops:
  0.0 0.0 copy-start
  0.0 1.5 %copy-done = bf16[1536,640]{1,0:T(8,128)(2,1)S(1)} copy-done((bf16[1536,640]{1,0:T(8,128)(2,1)S(1)}, bf16[1536,640]{1,0:T(8,128)(2,1)}, u32[]{:S(2)}) %copy-start) | copy-done | bytes 1966104
  1.5 3.3 %multiply_convert_fusion = bf16[640,640]{1,0:T(8,128)(2,1)S(1)} fusion(bf16[1536,640]{1,0:T(8,128)(2,1)S(1)} %copy-done, bf16[1536,640]{1,0:T(8,128)(2,1)} %param.3), kind=kOutput, calls=%fused_computation | convolution fusion | flops 1259110400 | bytes 4751360 | tf_op jit(solution)/shard_map/product/dot_general | solution.py:154
  4.8 28.4 %all_to_all.20 = bf16[4,160,640]{2,1,0:T(8,128)(2,1)S(1)} all-to-all(bf16[4,160,640]{2,1,0:T(8,128)(2,1)S(1)} %bitcast.9), channel_id=1, replica_groups={{0,16,32,48},{64,80,96,112},{128,144,160,176},{192,208,224,240},{256,27..., dimensions={0} | all-to-all | bytes 1638400 | tf_op jit(solution)/shard_map/near_sum/all_to_all | solution.py:135
  33.2 0.1 reduce_sum.24
  33.4 13.6 %all_to_all.21 = bf16[4,40,640]{2,1,0:T(8,128)(2,1)S(1)} all-to-all(bf16[4,40,640]{2,1,0:T(8,128)(2,1)S(1)} %bitcast.8), channel_id=1, replica_groups={{0,64,128,192},{16,80,144,208},{32,96,160,224},{48,112,176,240},{256,32..., dimensions={0} | all-to-all | bytes 409600 | tf_op jit(solution)/shard_map/middle_sum/all_to_all | solution.py:135
  46.9 1.3 %collective-permute-start.2 = (bf16[40,640]{1,0:T(8,128)(2,1)S(1)}, bf16[40,640]{1,0:T(8,128)(2,1)S(1)}, u32[]{:S(2)}, u32[]{:S(2)}) collective-permute-start(bf16[40,640]{1,0:T(8,128)(2,1)S(1)} %reduce_sum.25), channel_id=1, source_target_pairs={{512,0},{528,16},{544,32},{560,48},{576,64},{592,80},{608,96},{624... | collective-permute-start | bytes 153608 | tf_op jit(solution)/shard_map/far_sum/ppermute | solution.py:125
  48.2 1.3 %collective-permute-start.1 = (bf16[40,640]{1,0:T(8,128)(2,1)S(1)}, bf16[40,640]{1,0:T(8,128)(2,1)S(1)}, u32[]{:S(2)}, u32[]{:S(2)}) collective-permute-start(bf16[40,640]{1,0:T(8,128)(2,1)S(1)} %reduce_sum.25), channel_id=1, source_target_pairs={{768,0},{784,16},{800,32},{816,48},{832,64},{848,80},{864,96},{880... | collective-permute-start | bytes 153608 | tf_op jit(solution)/shard_map/far_sum/ppermute | solution.py:125
  49.5 1.3 %collective-permute-start = (bf16[40,640]{1,0:T(8,128)(2,1)S(1)}, bf16[40,640]{1,0:T(8,128)(2,1)S(1)}, u32[]{:S(2)}, u32[]{:S(2)}) collective-permute-start(bf16[40,640]{1,0:T(8,128)(2,1)S(1)} %reduce_sum.25), channel_id=1, source_target_pairs={{256,0},{272,16},{288,32},{304,48},{320,64},{336,80},{352,96},{368... | collective-permute-start | bytes 153608 | tf_op jit(solution)/shard_map/far_sum/ppermute | solution.py:125
  50.8 19.4 %collective-permute-done.2 = bf16[40,640]{1,0:T(8,128)(2,1)S(1)} collective-permute-done((bf16[40,640]{1,0:T(8,128)(2,1)S(1)}, bf16[40,640]{1,0:T(8,128)(2,1)S(1)}, u32[]{:S(2)}, u32[]{:S(2)}) %collective-permute-start.2) | collective-permute-done | bytes 51232 | tf_op jit(solution)/shard_map/far_sum/ppermute | solution.py:125
  70.2 0.0 collective-permute-done.1
  70.2 0.0 collective-permute-done
  70.3 1.7 %collective-permute-start.5 = (bf16[40,640]{1,0:T(8,128)(2,1)S(1)}, bf16[40,640]{1,0:T(8,128)(2,1)S(1)}, u32[]{:S(2)}, u32[]{:S(2)}) collective-permute-start(bf16[40,640]{1,0:T(8,128)(2,1)S(1)} %add_convert_fusion), channel_id=1, source_target_pairs={{0,512},{16,528},{32,544},{48,560},{64,576},{80,592},{96,608},{112... | collective-permute-start | bytes 153608 | tf_op jit(solution)/shard_map/far_sum/ppermute | solution.py:128
  72.0 1.3 %collective-permute-start.3 = (bf16[40,640]{1,0:T(8,128)(2,1)S(1)}, bf16[40,640]{1,0:T(8,128)(2,1)S(1)}, u32[]{:S(2)}, u32[]{:S(2)}) collective-permute-start(bf16[40,640]{1,0:T(8,128)(2,1)S(1)} %add_convert_fusion), channel_id=1, source_target_pairs={{0,256},{16,272},{32,288},{48,304},{64,320},{80,336},{96,352},{112... | collective-permute-start | bytes 153608 | tf_op jit(solution)/shard_map/far_sum/ppermute | solution.py:128
  73.3 1.3 %collective-permute-start.4 = (bf16[40,640]{1,0:T(8,128)(2,1)S(1)}, bf16[40,640]{1,0:T(8,128)(2,1)S(1)}, u32[]{:S(2)}, u32[]{:S(2)}) collective-permute-start(bf16[40,640]{1,0:T(8,128)(2,1)S(1)} %add_convert_fusion), channel_id=1, source_target_pairs={{0,768},{16,784},{32,800},{48,816},{64,832},{80,848},{96,864},{112... | collective-permute-start | bytes 153608 | tf_op jit(solution)/shard_map/far_sum/ppermute | solution.py:128
  74.6 0.0 collective-permute-done.5
  74.6 0.0 collective-permute-done.3
  74.6 8.3 %collective-permute-done.4 = bf16[40,640]{1,0:T(8,128)(2,1)S(1)} collective-permute-done((bf16[40,640]{1,0:T(8,128)(2,1)S(1)}, bf16[40,640]{1,0:T(8,128)(2,1)S(1)}, u32[]{:S(2)}, u32[]{:S(2)}) %collective-permute-start.4) | collective-permute-done | bytes 51232 | tf_op jit(solution)/shard_map/far_sum/ppermute | solution.py:128
  83.0 12.7 %all_to_all.22 = bf16[4,40,640]{2,1,0:T(8,128)(2,1)S(1)} all-to-all(bf16[4,40,640]{2,1,0:T(8,128)(2,1)S(1)} %broadcast_in_dim.6), channel_id=1, replica_groups={{0,64,128,192},{16,80,144,208},{32,96,160,224},{48,112,176,240},{256,32..., dimensions={0} | all-to-all | bytes 409600 | tf_op jit(solution)/shard_map/middle_gather/all_to_all | solution.py:135
  95.7 0.1 broadcast_in_dim.15
  95.7 17.1 %all_to_all.23 = bf16[4,160,640]{2,1,0:T(8,128)(2,1)S(1)} all-to-all(bf16[4,160,640]{2,1,0:T(8,128)(2,1)S(1)} %broadcast_in_dim.15), channel_id=1, replica_groups={{0,16,32,48},{64,80,96,112},{128,144,160,176},{192,208,224,240},{256,27..., dimensions={0} | all-to-all | bytes 1638400 | tf_op jit(solution)/shard_map/near_gather/all_to_all | solution.py:135
  112.8 5.7 %precondition.1 = f32[10,1,640]{2,1,0:T(1,128)} custom-call(bf16[640,640]{1,0:T(8,128)(2,1)S(1)} %bitcast.7), custom_call_target="tpu_custom_call" | custom-call | flops 3145728000 | bytes 819200 | tf_op jit(solution)/shard_map/precondition/pallas_call | solution.py:84
  (4 shorter events, 0.1 us)
Async XLA Ops:
  0.0 1.5 %copy-start = (bf16[1536,640]{1,0:T(8,128)(2,1)S(1)}, bf16[1536,640]{1,0:T(8,128)(2,1)}, u32[]{:S(2)}) copy-start(bf16[1536,640]{1,0:T(8,128)(2,1)} %param.2) | copy-start | bytes 5898244
  46.9 23.3 %collective-permute-start.2 = (bf16[40,640]{1,0:T(8,128)(2,1)S(1)}, bf16[40,640]{1,0:T(8,128)(2,1)S(1)}, u32[]{:S(2)}, u32[]{:S(2)}) collective-permute-start(bf16[40,640]{1,0:T(8,128)(2,1)S(1)} %reduce_sum.25), channel_id=1, source_target_pairs={{512,0},{528,16},{544,32},{560,48},{576,64},{592,80},{608,96},{624... | collective-permute-start | bytes 153608 | tf_op jit(solution)/shard_map/far_sum/ppermute | solution.py:125
  48.2 22.0 %collective-permute-start.1 = (bf16[40,640]{1,0:T(8,128)(2,1)S(1)}, bf16[40,640]{1,0:T(8,128)(2,1)S(1)}, u32[]{:S(2)}, u32[]{:S(2)}) collective-permute-start(bf16[40,640]{1,0:T(8,128)(2,1)S(1)} %reduce_sum.25), channel_id=1, source_target_pairs={{768,0},{784,16},{800,32},{816,48},{832,64},{848,80},{864,96},{880... | collective-permute-start | bytes 153608 | tf_op jit(solution)/shard_map/far_sum/ppermute | solution.py:125
  49.5 20.7 %collective-permute-start = (bf16[40,640]{1,0:T(8,128)(2,1)S(1)}, bf16[40,640]{1,0:T(8,128)(2,1)S(1)}, u32[]{:S(2)}, u32[]{:S(2)}) collective-permute-start(bf16[40,640]{1,0:T(8,128)(2,1)S(1)} %reduce_sum.25), channel_id=1, source_target_pairs={{256,0},{272,16},{288,32},{304,48},{320,64},{336,80},{352,96},{368... | collective-permute-start | bytes 153608 | tf_op jit(solution)/shard_map/far_sum/ppermute | solution.py:125
  70.3 4.4 %collective-permute-start.5 = (bf16[40,640]{1,0:T(8,128)(2,1)S(1)}, bf16[40,640]{1,0:T(8,128)(2,1)S(1)}, u32[]{:S(2)}, u32[]{:S(2)}) collective-permute-start(bf16[40,640]{1,0:T(8,128)(2,1)S(1)} %add_convert_fusion), channel_id=1, source_target_pairs={{0,512},{16,528},{32,544},{48,560},{64,576},{80,592},{96,608},{112... | collective-permute-start | bytes 153608 | tf_op jit(solution)/shard_map/far_sum/ppermute | solution.py:128
  72.0 2.7 %collective-permute-start.3 = (bf16[40,640]{1,0:T(8,128)(2,1)S(1)}, bf16[40,640]{1,0:T(8,128)(2,1)S(1)}, u32[]{:S(2)}, u32[]{:S(2)}) collective-permute-start(bf16[40,640]{1,0:T(8,128)(2,1)S(1)} %add_convert_fusion), channel_id=1, source_target_pairs={{0,256},{16,272},{32,288},{48,304},{64,320},{80,336},{96,352},{112... | collective-permute-start | bytes 153608 | tf_op jit(solution)/shard_map/far_sum/ppermute | solution.py:128
  73.3 9.7 %collective-permute-start.4 = (bf16[40,640]{1,0:T(8,128)(2,1)S(1)}, bf16[40,640]{1,0:T(8,128)(2,1)S(1)}, u32[]{:S(2)}, u32[]{:S(2)}) collective-permute-start(bf16[40,640]{1,0:T(8,128)(2,1)S(1)} %add_convert_fusion), channel_id=1, source_target_pairs={{0,768},{16,784},{32,800},{48,816},{64,832},{80,848},{96,864},{112... | collective-permute-start | bytes 153608 | tf_op jit(solution)/shard_map/far_sum/ppermute | solution.py:128

commit v7 on v6

--- a/solution.py
+++ b/solution.py
@@ -125,7 +125,7 @@
     for received in [lax.ppermute(part, axes, link) for link in links]:
         total += received.astype(jnp.float32)
     total = total.astype(jnp.bfloat16)
-    returned = [lax.ppermute(total, axes, [(b, a) for a, b in link]) for link in links]
+    returned = [lax.ppermute(total, axes, [(b, a) for a, b in link]) for link in links[::-1]]
     shift = jnp.where(lax.axis_index("blk") % 2 == 0, core_shifts[0], core_shifts[1])
     first = (lax.axis_index("dp") // 2 - shift) % (count // 2) < 8
     return jnp.where(first, total, functools.reduce(jnp.add, returned))

time: 119 us -> 120 us (level)
  blocking collectives: 71.7 us -> 80.2 us
  waiting for transfers between devices: 27.7 us -> 20.5 us
    all_to_all x4, blocking collectives: 71.7 us -> 80.2 us  [exchange(): return lax.all_to_all(parts, axes, 0, 0, axis_index_groups=groups)]
    ppermute x3, waiting for transfers between devices: 8.31 us -> 1.12 us  [far_sum(): lax.ppermute(total, axes, [(b, a) for a, b in link])]
where the time goes in v7:
time: 120 us; the launch traced here: 119 us
  blocking collectives  80.2 us (67%)
  waiting for transfers between devices  20.5 us (17%)
  starting transfers between devices  7.75 us (6%)
  Pallas kernels  5.67 us (5%)
  matrix products  3.28 us (3%)
  local copies, waits for them, and re-layouts  1.63 us (1%)
    all_to_all x4, blocking collectives, exchange(): return lax.all_to_all(parts, axes, 0, 0, axis_index_groups=groups)  80.2 us
    ppermute x3, waiting for transfers between devices, far_sum(): lax.ppermute(part, axes, link)  19.4 us
    pallas_call x1, Pallas kernels, precondition(): pl.pallas_call(precondition_kernel, out_shape=jax.ShapeDtypeStruct((slab_...  5.67 us
    ppermute x3, starting transfers between devices, far_sum(): lax.ppermute(total, axes, [(b, a) for a, b in link])  3.88 us
    ppermute x3, starting transfers between devices, far_sum(): lax.ppermute(part, axes, link)  3.88 us
    dot_general x1, matrix products, per_device(): lax.dot_general(activations, cotangent, (((0,), (0,)), ((), ())), preferr...  3.28 us
  transfers between devices with their start and end apart: 6, of which 2 were waited for; matrix products, arithmetic and copies ran while one was open for 0% of the time, Pallas kernels for 0%

profile of v7, /device:TPU:1, one launch (start us, length us, event | category | flops | bytes accessed | tf_op | source)
XLA Modules:
  0.0 119.3 jit_solution(13703870263561207980)
XLA Ops:
  0.0 0.0 copy-start
  0.0 1.5 %copy-done = bf16[1536,640]{1,0:T(8,128)(2,1)S(1)} copy-done((bf16[1536,640]{1,0:T(8,128)(2,1)S(1)}, bf16[1536,640]{1,0:T(8,128)(2,1)}, u32[]{:S(2)}) %copy-start) | copy-done | bytes 1966104
  1.5 3.3 %multiply_convert_fusion = bf16[640,640]{1,0:T(8,128)(2,1)S(1)} fusion(bf16[1536,640]{1,0:T(8,128)(2,1)S(1)} %copy-done, bf16[1536,640]{1,0:T(8,128)(2,1)} %param.3), kind=kOutput, calls=%fused_computation | convolution fusion | flops 1259110400 | bytes 4751360 | tf_op jit(solution)/shard_map/product/dot_general | solution.py:154
  4.8 28.4 %all_to_all.20 = bf16[4,160,640]{2,1,0:T(8,128)(2,1)S(1)} all-to-all(bf16[4,160,640]{2,1,0:T(8,128)(2,1)S(1)} %bitcast.9), channel_id=1, replica_groups={{0,16,32,48},{64,80,96,112},{128,144,160,176},{192,208,224,240},{256,27..., dimensions={0} | all-to-all | bytes 1638400 | tf_op jit(solution)/shard_map/near_sum/all_to_all | solution.py:135
  33.2 0.1 reduce_sum.24
  33.4 13.6 %all_to_all.21 = bf16[4,40,640]{2,1,0:T(8,128)(2,1)S(1)} all-to-all(bf16[4,40,640]{2,1,0:T(8,128)(2,1)S(1)} %bitcast.8), channel_id=1, replica_groups={{0,64,128,192},{16,80,144,208},{32,96,160,224},{48,112,176,240},{256,32..., dimensions={0} | all-to-all | bytes 409600 | tf_op jit(solution)/shard_map/middle_sum/all_to_all | solution.py:135
  46.9 1.3 %collective-permute-start.2 = (bf16[40,640]{1,0:T(8,128)(2,1)S(1)}, bf16[40,640]{1,0:T(8,128)(2,1)S(1)}, u32[]{:S(2)}, u32[]{:S(2)}) collective-permute-start(bf16[40,640]{1,0:T(8,128)(2,1)S(1)} %reduce_sum.25), channel_id=1, source_target_pairs={{512,0},{528,16},{544,32},{560,48},{576,64},{592,80},{608,96},{624... | collective-permute-start | bytes 153608 | tf_op jit(solution)/shard_map/far_sum/ppermute | solution.py:125
  48.2 1.3 %collective-permute-start.1 = (bf16[40,640]{1,0:T(8,128)(2,1)S(1)}, bf16[40,640]{1,0:T(8,128)(2,1)S(1)}, u32[]{:S(2)}, u32[]{:S(2)}) collective-permute-start(bf16[40,640]{1,0:T(8,128)(2,1)S(1)} %reduce_sum.25), channel_id=1, source_target_pairs={{768,0},{784,16},{800,32},{816,48},{832,64},{848,80},{864,96},{880... | collective-permute-start | bytes 153608 | tf_op jit(solution)/shard_map/far_sum/ppermute | solution.py:125
  49.5 1.3 %collective-permute-start = (bf16[40,640]{1,0:T(8,128)(2,1)S(1)}, bf16[40,640]{1,0:T(8,128)(2,1)S(1)}, u32[]{:S(2)}, u32[]{:S(2)}) collective-permute-start(bf16[40,640]{1,0:T(8,128)(2,1)S(1)} %reduce_sum.25), channel_id=1, source_target_pairs={{256,0},{272,16},{288,32},{304,48},{320,64},{336,80},{352,96},{368... | collective-permute-start | bytes 153608 | tf_op jit(solution)/shard_map/far_sum/ppermute | solution.py:125
  50.8 19.4 %collective-permute-done.2 = bf16[40,640]{1,0:T(8,128)(2,1)S(1)} collective-permute-done((bf16[40,640]{1,0:T(8,128)(2,1)S(1)}, bf16[40,640]{1,0:T(8,128)(2,1)S(1)}, u32[]{:S(2)}, u32[]{:S(2)}) %collective-permute-start.2) | collective-permute-done | bytes 51232 | tf_op jit(solution)/shard_map/far_sum/ppermute | solution.py:125
  70.2 0.0 collective-permute-done.1
  70.2 0.0 collective-permute-done
  70.3 1.3 %collective-permute-start.5 = (bf16[40,640]{1,0:T(8,128)(2,1)S(1)}, bf16[40,640]{1,0:T(8,128)(2,1)S(1)}, u32[]{:S(2)}, u32[]{:S(2)}) collective-permute-start(bf16[40,640]{1,0:T(8,128)(2,1)S(1)} %add_convert_fusion), channel_id=1, source_target_pairs={{0,256},{16,272},{32,288},{48,304},{64,320},{80,336},{96,352},{112... | collective-permute-start | bytes 153608 | tf_op jit(solution)/shard_map/far_sum/ppermute | solution.py:128
  71.6 1.3 %collective-permute-start.3 = (bf16[40,640]{1,0:T(8,128)(2,1)S(1)}, bf16[40,640]{1,0:T(8,128)(2,1)S(1)}, u32[]{:S(2)}, u32[]{:S(2)}) collective-permute-start(bf16[40,640]{1,0:T(8,128)(2,1)S(1)} %add_convert_fusion), channel_id=1, source_target_pairs={{0,512},{16,528},{32,544},{48,560},{64,576},{80,592},{96,608},{112... | collective-permute-start | bytes 153608 | tf_op jit(solution)/shard_map/far_sum/ppermute | solution.py:128
  72.9 1.3 %collective-permute-start.4 = (bf16[40,640]{1,0:T(8,128)(2,1)S(1)}, bf16[40,640]{1,0:T(8,128)(2,1)S(1)}, u32[]{:S(2)}, u32[]{:S(2)}) collective-permute-start(bf16[40,640]{1,0:T(8,128)(2,1)S(1)} %add_convert_fusion), channel_id=1, source_target_pairs={{0,768},{16,784},{32,800},{48,816},{64,832},{80,848},{96,864},{112... | collective-permute-start | bytes 153608 | tf_op jit(solution)/shard_map/far_sum/ppermute | solution.py:128
  74.2 0.0 collective-permute-done.5
  74.2 0.0 collective-permute-done.3
  74.2 1.1 collective-permute-done.4
  75.4 18.6 %all_to_all.22 = bf16[4,40,640]{2,1,0:T(8,128)(2,1)S(1)} all-to-all(bf16[4,40,640]{2,1,0:T(8,128)(2,1)S(1)} %broadcast_in_dim.6), channel_id=1, replica_groups={{0,64,128,192},{16,80,144,208},{32,96,160,224},{48,112,176,240},{256,32..., dimensions={0} | all-to-all | bytes 409600 | tf_op jit(solution)/shard_map/middle_gather/all_to_all | solution.py:135
  94.0 0.1 broadcast_in_dim.15
  94.0 19.6 %all_to_all.23 = bf16[4,160,640]{2,1,0:T(8,128)(2,1)S(1)} all-to-all(bf16[4,160,640]{2,1,0:T(8,128)(2,1)S(1)} %broadcast_in_dim.15), channel_id=1, replica_groups={{0,16,32,48},{64,80,96,112},{128,144,160,176},{192,208,224,240},{256,27..., dimensions={0} | all-to-all | bytes 1638400 | tf_op jit(solution)/shard_map/near_gather/all_to_all | solution.py:135
  113.7 5.7 %precondition.1 = f32[10,1,640]{2,1,0:T(1,128)} custom-call(bf16[640,640]{1,0:T(8,128)(2,1)S(1)} %bitcast.7), custom_call_target="tpu_custom_call" | custom-call | flops 3145728000 | bytes 819200 | tf_op jit(solution)/shard_map/precondition/pallas_call | solution.py:84
  (4 shorter events, 0.1 us)
Async XLA Ops:
  0.0 1.5 %copy-start = (bf16[1536,640]{1,0:T(8,128)(2,1)S(1)}, bf16[1536,640]{1,0:T(8,128)(2,1)}, u32[]{:S(2)}) copy-start(bf16[1536,640]{1,0:T(8,128)(2,1)} %param.2) | copy-start | bytes 5898244
  46.9 23.3 %collective-permute-start.2 = (bf16[40,640]{1,0:T(8,128)(2,1)S(1)}, bf16[40,640]{1,0:T(8,128)(2,1)S(1)}, u32[]{:S(2)}, u32[]{:S(2)}) collective-permute-start(bf16[40,640]{1,0:T(8,128)(2,1)S(1)} %reduce_sum.25), channel_id=1, source_target_pairs={{512,0},{528,16},{544,32},{560,48},{576,64},{592,80},{608,96},{624... | collective-permute-start | bytes 153608 | tf_op jit(solution)/shard_map/far_sum/ppermute | solution.py:125
  48.2 22.0 %collective-permute-start.1 = (bf16[40,640]{1,0:T(8,128)(2,1)S(1)}, bf16[40,640]{1,0:T(8,128)(2,1)S(1)}, u32[]{:S(2)}, u32[]{:S(2)}) collective-permute-start(bf16[40,640]{1,0:T(8,128)(2,1)S(1)} %reduce_sum.25), channel_id=1, source_target_pairs={{768,0},{784,16},{800,32},{816,48},{832,64},{848,80},{864,96},{880... | collective-permute-start | bytes 153608 | tf_op jit(solution)/shard_map/far_sum/ppermute | solution.py:125
  49.5 20.7 %collective-permute-start = (bf16[40,640]{1,0:T(8,128)(2,1)S(1)}, bf16[40,640]{1,0:T(8,128)(2,1)S(1)}, u32[]{:S(2)}, u32[]{:S(2)}) collective-permute-start(bf16[40,640]{1,0:T(8,128)(2,1)S(1)} %reduce_sum.25), channel_id=1, source_target_pairs={{256,0},{272,16},{288,32},{304,48},{320,64},{336,80},{352,96},{368... | collective-permute-start | bytes 153608 | tf_op jit(solution)/shard_map/far_sum/ppermute | solution.py:125
  70.3 3.9 %collective-permute-start.5 = (bf16[40,640]{1,0:T(8,128)(2,1)S(1)}, bf16[40,640]{1,0:T(8,128)(2,1)S(1)}, u32[]{:S(2)}, u32[]{:S(2)}) collective-permute-start(bf16[40,640]{1,0:T(8,128)(2,1)S(1)} %add_convert_fusion), channel_id=1, source_target_pairs={{0,256},{16,272},{32,288},{48,304},{64,320},{80,336},{96,352},{112... | collective-permute-start | bytes 153608 | tf_op jit(solution)/shard_map/far_sum/ppermute | solution.py:128
  71.6 2.7 %collective-permute-start.3 = (bf16[40,640]{1,0:T(8,128)(2,1)S(1)}, bf16[40,640]{1,0:T(8,128)(2,1)S(1)}, u32[]{:S(2)}, u32[]{:S(2)}) collective-permute-start(bf16[40,640]{1,0:T(8,128)(2,1)S(1)} %add_convert_fusion), channel_id=1, source_target_pairs={{0,512},{16,528},{32,544},{48,560},{64,576},{80,592},{96,608},{112... | collective-permute-start | bytes 153608 | tf_op jit(solution)/shard_map/far_sum/ppermute | solution.py:128
  72.9 2.5 %collective-permute-start.4 = (bf16[40,640]{1,0:T(8,128)(2,1)S(1)}, bf16[40,640]{1,0:T(8,128)(2,1)S(1)}, u32[]{:S(2)}, u32[]{:S(2)}) collective-permute-start(bf16[40,640]{1,0:T(8,128)(2,1)S(1)} %add_convert_fusion), channel_id=1, source_target_pairs={{0,768},{16,784},{32,800},{48,816},{64,832},{80,848},{96,864},{112... | collective-permute-start | bytes 153608 | tf_op jit(solution)/shard_map/far_sum/ppermute | solution.py:128
